TPU v7x, 32 devices: a whole 2x2x4 slice. The times are simulated.
32 devices in a mesh: section: 2 (over y), seq: 16 (over z, x, core).
Axes of the slice: x: 2, y: 2, z: 4, core: 2. Of those that a mesh axis runs over, the one named last changes fastest.
Arguments:
- activations: bfloat16 [2, 2048, 3584], P('section', 'seq'), may hold values from -80 to 80
- incoming: bfloat16 [2048, 3584], P('seq'), may hold values from -4 to 4
- column_ids: int32 [3, 2048], replicated, may hold values from 0 to 11, as said below
- positions: int32 [3, 2048], replicated, may hold values from 0 to 23, as said below
- norm_gain: float32 [2, 3584], P('section')
- w_query: bfloat16 [2, 3584, 1792], P('section', 'seq')
- w_key: bfloat16 [2, 3584, 256], P('section', 'seq')
- w_value: bfloat16 [2, 3584, 256], P('section', 'seq'), may hold values from -0.09375 to 0.09375
- w_out: bfloat16 [2, 1792, 3584], P('section', 'seq'), may hold values from -0.125 to 0.125
- b_query: float32 [2, 1792], P('section'), may hold values from -4 to 4
- b_key: float32 [2, 256], P('section'), may hold values from -4 to 4
- b_value: float32 [2, 256], P('section'), may hold values from -3 to 3
Outputs:
- first_pass: bfloat16 [2, 2048, 3584], P('section', 'seq')
- second_pass: bfloat16 [2, 2048, 3584], P('section', 'seq')
Inputs may be any that keep to these rules, and one draw needn't show every extreme that they name: `column_ids`: each row is one serialized table: runs of one or two consecutive tokens form cells, the cells take the column numbers 0, 1, ..., 11 in turn, table row after table row; column 0 is a row's header cell. The first table row of every micro-batch has two tokens in each cell. `positions`: A token's position counts the tokens since its table row began.
All inputs are finite; a program needn't handle non-finite values.
Results may differ from a plain program's by a relative error of at most 0.012.
Values may be sent and summed in bfloat16 or wider, within the bound.
A program may use at most 128 MiB of HBM per device.

v0:
```python
import jax
import jax.numpy as jnp
from jax import lax
from jax.sharding import PartitionSpec as P

HEAD_DIM = 128
HEADS = 14
KV_HEADS = 2


EPSILON = 1e-06
THETA = 1000000.0


def from_behind(value, axis, by):
    length = lax.axis_size(axis)
    pairs = [(i, i + by) for i in range(length) if 0 <= i + by < length]
    return lax.ppermute(value, axis, pairs)


def rotate(entries, places):
    half = entries.shape[-1] // 2
    freqs = THETA ** (-(jnp.arange(half, dtype=jnp.float32) * 2.0) / entries.shape[-1])
    angles = places.astype(jnp.float32)[:, None] * freqs[None, :]
    cosine = jnp.cos(angles)[:, None, :]
    sine = jnp.sin(angles)[:, None, :]
    first = entries[..., :half]
    second = entries[..., half:]
    return jnp.concatenate(
        [first * cosine - second * sine, second * cosine + first * sine], axis=-1
    )


def normalize(inputs, gain):
    wide = inputs.astype(jnp.float32)
    hidden = (
        wide * lax.rsqrt(jnp.mean(wide * wide, axis=-1, keepdims=True) + EPSILON) * gain
    ).astype(jnp.bfloat16)
    return (wide, hidden)


def per_device(
    activations,
    incoming,
    column_ids,
    positions,
    norm_gain,
    w_query,
    w_key,
    w_value,
    w_out,
    b_query,
    b_key,
    b_value,
):
    section_index = lax.axis_index("section")
    section_count = lax.axis_size("section")
    shard_index = lax.axis_index("seq")
    rows_dev = activations.shape[1]
    group = HEADS // KV_HEADS
    scale = HEAD_DIM ** (-0.5)
    gain = norm_gain[0]
    query_bias = b_query[0]
    key_bias = b_key[0]
    value_bias = b_value[0]
    query_index = shard_index * rows_dev + jnp.arange(rows_dev, dtype=jnp.int32)
    second_row = (section_index + section_count) % (section_count + 1)

    def finish(query_sum, key_sum, value_sum, micro_row):
        places_all = lax.dynamic_index_in_dim(positions, micro_row, 0, keepdims=False)
        places = lax.dynamic_slice_in_dim(places_all, shard_index * rows_dev, rows_dev)
        queries = rotate(
            (query_sum + query_bias).reshape(rows_dev, HEADS, HEAD_DIM), places
        ).astype(jnp.bfloat16)
        keys_rot = rotate(
            (key_sum + key_bias).reshape(rows_dev, KV_HEADS, HEAD_DIM), places
        ).astype(jnp.bfloat16)
        values = (value_sum + value_bias).astype(jnp.bfloat16).reshape(rows_dev, KV_HEADS, HEAD_DIM)
        return (queries, keys_rot, values)

    def attend(queries, keys_rot, values, micro_row):
        columns = lax.dynamic_index_in_dim(column_ids, micro_row, 0, keepdims=False)
        query_cols = lax.dynamic_slice_in_dim(columns, shard_index * rows_dev, rows_dev)
        query_grouped = queries.reshape(rows_dev, KV_HEADS, group, HEAD_DIM)
        top = jnp.full((KV_HEADS, group, rows_dev), -1e30, jnp.float32)
        key_piece = lax.all_gather(keys_rot, "seq", axis=0, tiled=True)
        value_piece = lax.all_gather(values, "seq", axis=0, tiled=True)
        count = key_piece.shape[0]
        key_index = jnp.arange(count, dtype=jnp.int32)
        allowed = (key_index[None, :] <= query_index[:, None]) & (
            (columns[None, :] == query_cols[:, None]) | (columns[None, :] == 0)
        )
        scores = (
            jnp.einsum(
                "qhgd,khd->hgqk", query_grouped, key_piece, preferred_element_type=jnp.float32
            )
            * scale
        )
        scores = jnp.where(allowed[None, None], scores, -1e30)
        new_top = jnp.maximum(top, jnp.max(scores, axis=-1))
        exponentials = jnp.where(allowed[None, None], jnp.exp(scores - new_top[..., None]), 0.0)
        total = jnp.sum(exponentials, axis=-1)
        probs = exponentials.astype(jnp.bfloat16)
        summed = jnp.einsum(
            "hgqk,khd->hgqd", probs, value_piece, preferred_element_type=jnp.float32
        )
        top, total, summed = (new_top, total, summed)
        mixed = summed / total[..., None]
        return (
            jnp.transpose(mixed, (2, 0, 1, 3))
            .reshape(rows_dev, HEADS * HEAD_DIM)
            .astype(jnp.bfloat16)
        )

    first_wide, first_hidden = normalize(activations[0], gain)
    full_query, full_key, full_value, full_out = (
        lax.all_gather(w_query[0], "seq", axis=0, tiled=True),
        lax.all_gather(w_key[0], "seq", axis=0, tiled=True),
        lax.all_gather(w_value[0], "seq", axis=0, tiled=True),
        lax.all_gather(w_out[0], "seq", axis=0, tiled=True),
    )
    query_sum = jnp.dot(first_hidden, full_query, preferred_element_type=jnp.float32)
    key_sum = jnp.dot(first_hidden, full_key, preferred_element_type=jnp.float32)
    value_sum = jnp.dot(first_hidden, full_value, preferred_element_type=jnp.float32)
    queries, keys_rot, values = finish(query_sum, key_sum, value_sum, section_index)
    context = attend(queries, keys_rot, values, section_index)
    first_out = (
        first_wide + jnp.dot(context, full_out, preferred_element_type=jnp.float32)
    ).astype(jnp.bfloat16)
    passed = from_behind(first_out, "section", 1)
    second_in = jnp.where(section_index == 0, incoming, passed)
    second_wide, second_hidden = normalize(second_in, gain)
    query_next = jnp.dot(second_hidden, full_query, preferred_element_type=jnp.float32)
    key_next = jnp.dot(second_hidden, full_key, preferred_element_type=jnp.float32)
    value_next = jnp.dot(second_hidden, full_value, preferred_element_type=jnp.float32)
    queries_two, keys_two, values_two = finish(query_next, key_next, value_next, second_row)
    context_two = attend(queries_two, keys_two, values_two, second_row)
    second_out = (
        second_wide + jnp.dot(context_two, full_out, preferred_element_type=jnp.float32)
    ).astype(jnp.bfloat16)
    return (first_out[None], second_out[None])


def solution(mesh):
    placed = (
        P("section", "seq", None),
        P("seq", None),
        P(),
        P(),
        P("section", None),
        P("section", "seq", None),
        P("section", "seq", None),
        P("section", "seq", None),
        P("section", "seq", None),
        P("section", None),
        P("section", None),
        P("section", None),
    )
    return jax.shard_map(
        per_device,
        mesh=mesh,
        in_specs=placed,
        out_specs=(P("section", "seq", None), P("section", "seq", None)),
        check_vma=False,
    )
```

profile of v0, /device:TPU:29, one launch (start us, length us, event | category | flops | bytes accessed | tf_op | source)
XLA Modules:
  0.0 510.6 jit_solution(12638923284492024392)
XLA Ops:
  13.1 37.9 %all-gather.21.cloned.1.call-done = bf16[1,3584,256]{2,1,0:T(8,128)(2,1)} async-done(((bf16[1,224,256]{2,1,0:T(8,128)(2,1)}), bf16[1,3584,256]{2,1,0:T(8,128)(2,1)}) %all-gather.21.cloned.1.call-update) | async-done | bytes 1835024 | tf_op jit(solution)/shard_map/all_gather | solution.py:118
  51.0 2.2 fusion.61
  54.3 38.3 %all-gather.25.cloned.1.call-done = bf16[1,3584,256]{2,1,0:T(8,128)(2,1)} async-done(((bf16[1,224,256]{2,1,0:T(8,128)(2,1)}), bf16[1,3584,256]{2,1,0:T(8,128)(2,1)}) %all-gather.25.cloned.1.call-update) | async-done | bytes 1835024 | tf_op jit(solution)/shard_map/all_gather | solution.py:119
  92.5 2.2 fusion.76
  97.8 2.1 fusion.85
  99.8 95.5 %all-gather.23.cloned.1.call-done = bf16[1,3584,1792]{2,1,0:T(8,128)(2,1)} async-done(((bf16[1,224,1792]{2,1,0:T(8,128)(2,1)}), bf16[1,3584,1792]{2,1,0:T(8,128)(2,1)}) %all-gather.23.cloned.1.call-update) | async-done | bytes 12845072 | tf_op jit(solution)/shard_map/all_gather | solution.py:117
  195.4 6.5 %fusion.35 = f32[128,1792]{1,0:T(8,128)S(1)} fusion(bf16[1,3584,1792]{2,1,0:T(8,128)(2,1)} %all-gather.23.cloned.1.call-done, f32[1792]{0:T(1024)S(1)} %reduce.2, bf16[1,128,3584]{2,1,0:T(8,128)(2,1)S(1)} %copy-done, f32[3584]{0:T(1024)S(1)} %reduce, f32[128]{0:T(128)S(1)} %add_rsqrt_fusion.1), kind=kOutput, calls=%fused_computation.31 | convolution fusion | flops 1646231552 | bytes 14702080 | tf_op jit(solution)/shard_map/dot_general | solution.py:122
  202.9 32.0 %all-gather.13.cloned.1.call-done = bf16[2048,2,128]{2,0,1:T(8,128)(2,1)} async-done(((bf16[128,2,128]{2,0,1:T(8,128)(2,1)}), bf16[2048,2,128]{2,0,1:T(8,128)(2,1)}) %all-gather.13.cloned.1.call-update) | async-done | bytes 1048592 | tf_op jit(solution)/shard_map/all_gather | solution.py:86
  235.0 8.8 %fusion = (f32[2,7,128]{2,1,0:T(8,128)S(1)}, f32[2,2048,128,7]{2,1,3,0:T(8,128)}) fusion(pred[128,2048]{0,1:T(8,128)(4,1)S(1)} %get-tuple-element.31, bf16[128,2,7,64]{3,0,2,1:T(8,128)(2,1)S(1)} %bitcast.166, bf16[128,2,7,64]{3,0,2,1:T(8,128)(2,1)S(1)} %bitcast.165, bf16[2048,2,128]{2,0,1:T(8,128)(2,1)} %all-gather.13.cloned.1.call-done), kind=kOutput, calls=%fused_computation.4 | convolution fusion | flops 951449856 | bytes 16456704 | tf_op jit(solution)/shard_map/qhgd,khd->hgqk/dot_general | solution.py:94
  243.7 8.6 %fusion.10 = f32[2,7,128]{2,1,0:T(8,128)S(1)} fusion(f32[2,2048,128,7]{2,1,3,0:T(8,128)} %get-tuple-element.35, f32[2,7,128]{2,1,0:T(8,128)S(1)} %broadcast_maximum_fusion.1, pred[128,2048]{0,1:T(8,128)(4,1)S(1)} %get-tuple-element.31), kind=kLoop, calls=%fused_computation.14 | loop fusion | flops 18348288 | bytes 14956544 | tf_op jit(solution)/shard_map/reduce_sum | solution.py:102
  252.4 20.6 %all-gather.15.cloned.1.call-done = bf16[2048,2,128]{0,2,1:T(8,128)(2,1)} async-done(((bf16[128,2,128]{0,2,1:T(8,128)(2,1)}), bf16[2048,2,128]{0,2,1:T(8,128)(2,1)}) %all-gather.15.cloned.1.call-update) | async-done | bytes 1048592 | tf_op jit(solution)/shard_map/all_gather | solution.py:87
  273.0 9.3 %fusion.102 = bf16[128,2,7,128]{0,3,2,1:T(8,128)(2,1)S(1)} fusion(f32[2,2048,128,7]{2,1,3,0:T(8,128)} %get-tuple-element.35, f32[2,7,128]{2,1,0:T(8,128)S(1)} %broadcast_maximum_fusion.1, pred[128,2048]{0,1:T(8,128)(4,1)S(1)} %get-tuple-element.31, bf16[2048,2,128]{0,2,1:T(8,128)(2,1)} %all-gather.15.cloned.1.call-done, f32[128,2,7]{0,2,1:T(8,128)S(1)} %bitcast.173), kind=kOutput, calls=%fused_computation.67 | convolution fusion | flops 958332928 | bytes 16463872 | tf_op jit(solution)/shard_map/hgqk,khd->hgqd/dot_general | solution.py:104
  282.3 94.3 %all-gather.27.cloned.1.call-done = bf16[1,1792,3584]{2,1,0:T(8,128)(2,1)} async-done(((bf16[1,112,3584]{2,1,0:T(8,128)(2,1)}), bf16[1,1792,3584]{2,1,0:T(8,128)(2,1)}) %all-gather.27.cloned.1.call-update) | async-done | bytes 12845072 | tf_op jit(solution)/shard_map/all_gather | solution.py:120
  376.5 7.7 %fusion.29 = bf16[128,3584]{1,0:T(8,128)(2,1)} fusion(bf16[128,1792]{0,1:T(8,128)(2,1)S(1)} %bitcast.167, bf16[1,1792,3584]{2,1,0:T(8,128)(2,1)} %all-gather.27.cloned.1.call-done, bf16[1,128,3584]{2,1,0:T(8,128)(2,1)S(1)} %copy-done), kind=kOutput, calls=%fused_computation.25 | convolution fusion | flops 1645543424 | bytes 15138816 | tf_op jit(solution)/shard_map/dot_general | solution.py:128
  385.7 22.3 %collective-permute-done = bf16[128,3584]{1,0:T(8,128)(2,1)S(1)} collective-permute-done((bf16[128,3584]{1,0:T(8,128)(2,1)}, bf16[128,3584]{1,0:T(8,128)(2,1)S(1)}, u32[]{:S(2)}, u32[]{:S(2)}) %collective-permute-start) | collective-permute-done | bytes 917536 | tf_op jit(solution)/shard_map/ppermute | solution.py:18
  408.4 2.0 fusion.64
  411.5 6.5 %fusion.38 = f32[128,1792]{1,0:T(8,128)S(1)} fusion(bf16[1,3584,1792]{2,1,0:T(8,128)(2,1)} %all-gather.23.cloned.1.call-done, f32[1792]{0:T(1024)S(1)} %reduce.2, bf16[128,3584]{1,0:T(8,128)(2,1)S(1)} %get-tuple-element.5, f32[128]{0:T(128)S(1)} %add_rsqrt_fusion, f32[3584]{0:T(1024)S(1)} %reduce), kind=kOutput, calls=%fused_computation.32 | convolution fusion | flops 1646231552 | bytes 14702080 | tf_op jit(solution)/shard_map/dot_general | solution.py:133
  419.1 2.0 fusion.73
  421.8 27.6 %all-gather.17.cloned.1.call-done = bf16[2048,2,128]{2,0,1:T(8,128)(2,1)} async-done(((bf16[128,2,128]{2,0,1:T(8,128)(2,1)}), bf16[2048,2,128]{2,0,1:T(8,128)(2,1)}) %all-gather.17.cloned.1.call-update) | async-done | bytes 1048592 | tf_op jit(solution)/shard_map/all_gather | solution.py:86
  449.4 8.8 %fusion.1 = (f32[2,7,128]{2,1,0:T(8,128)S(1)}, f32[2,2048,128,7]{2,1,3,0:T(8,128)}) fusion(pred[128,2048]{0,1:T(8,128)(4,1)S(1)} %get-tuple-element.30, bf16[128,2,7,64]{3,0,2,1:T(8,128)(2,1)S(1)} %bitcast.164, bf16[128,2,7,64]{3,0,2,1:T(8,128)(2,1)S(1)} %bitcast.163, bf16[2048,2,128]{2,0,1:T(8,128)(2,1)} %all-gather.17.cloned.1.call-done), kind=kOutput, calls=%fused_computation.5 | convolution fusion | flops 951449856 | bytes 16456704 | tf_op jit(solution)/shard_map/qhgd,khd->hgqk/dot_general | solution.py:94
  458.2 8.6 %fusion.12 = f32[2,7,128]{2,1,0:T(8,128)S(1)} fusion(f32[2,2048,128,7]{2,1,3,0:T(8,128)} %get-tuple-element.37, f32[2,7,128]{2,1,0:T(8,128)S(1)} %broadcast_maximum_fusion, pred[128,2048]{0,1:T(8,128)(4,1)S(1)} %get-tuple-element.30), kind=kLoop, calls=%fused_computation.16 | loop fusion | flops 18348288 | bytes 14956544 | tf_op jit(solution)/shard_map/reduce_sum | solution.py:102
  466.8 20.1 %all-gather.19.cloned.1.call-done = bf16[2048,2,128]{0,2,1:T(8,128)(2,1)} async-done(((bf16[128,2,128]{0,2,1:T(8,128)(2,1)}), bf16[2048,2,128]{0,2,1:T(8,128)(2,1)}) %all-gather.19.cloned.1.call-update) | async-done | bytes 1048592 | tf_op jit(solution)/shard_map/all_gather | solution.py:87
  487.0 9.3 %fusion.92 = bf16[128,2,7,128]{0,3,2,1:T(8,128)(2,1)S(1)} fusion(f32[2,2048,128,7]{2,1,3,0:T(8,128)} %get-tuple-element.37, f32[2,7,128]{2,1,0:T(8,128)S(1)} %broadcast_maximum_fusion, pred[128,2048]{0,1:T(8,128)(4,1)S(1)} %get-tuple-element.30, bf16[2048,2,128]{0,2,1:T(8,128)(2,1)} %all-gather.19.cloned.1.call-done, f32[128,2,7]{0,2,1:T(8,128)S(1)} %bitcast.174), kind=kOutput, calls=%fused_computation.65 | convolution fusion | flops 958332928 | bytes 16463872 | tf_op jit(solution)/shard_map/hgqk,khd->hgqd/dot_general | solution.py:104
  496.3 7.5 %fusion.32 = bf16[1,128,3584]{2,1,0:T(8,128)(2,1)} fusion(bf16[128,1792]{0,1:T(8,128)(2,1)S(1)} %bitcast.168, bf16[1,1792,3584]{2,1,0:T(8,128)(2,1)} %all-gather.27.cloned.1.call-done, bf16[128,3584]{1,0:T(8,128)(2,1)S(1)} %get-tuple-element.5), kind=kOutput, calls=%fused_computation.26 | convolution fusion | flops 1645543424 | bytes 15138816 | tf_op jit(solution)/shard_map/dot_general | solution.py:139
  (60 shorter events, 15.6 us)
Async XLA Ops:
  7.2 188.2 %copy-start = (bf16[1,128,3584]{2,1,0:T(8,128)(2,1)S(1)}, bf16[1,128,3584]{2,1,0:T(8,128)(2,1)}, u32[]{:S(2)}) copy-start(bf16[1,128,3584]{2,1,0:T(8,128)(2,1)} %param.12) | copy-start | bytes 2752516
  7.2 43.8 %all-gather.21.cloned.1.call-start = ((), (), s32[]{:S(2)}) async-start(), calls=%async_computation.4 | async-start | bytes 1949696 | tf_op jit(solution)/shard_map/all_gather | solution.py:118
  7.9 84.6 %all-gather.25.cloned.1.call-start = ((), (), s32[]{:S(2)}) async-start(), calls=%async_computation.6 | async-start | bytes 1949696 | tf_op jit(solution)/shard_map/all_gather | solution.py:119
  8.7 186.7 %all-gather.23.cloned.1.call-start = ((), (), s32[]{:S(2)}) async-start(), calls=%async_computation.5 | async-start | bytes 13647872 | tf_op jit(solution)/shard_map/all_gather | solution.py:117
  9.4 225.6 %all-gather.13.cloned.1.call-start = ((), (), s32[]{:S(2)}) async-start(), calls=%async_computation | async-start | bytes 1114112 | tf_op jit(solution)/shard_map/all_gather | solution.py:86
  54.2 218.7 %all-gather.15.cloned.1.call-start = ((), (), s32[]{:S(2)}) async-start(), calls=%async_computation.1 | async-start | bytes 1114112 | tf_op jit(solution)/shard_map/all_gather | solution.py:87
  95.5 281.0 %all-gather.27.cloned.1.call-start = ((), (), s32[]{:S(2)}) async-start(), calls=%async_computation.7 | async-start | bytes 13647872 | tf_op jit(solution)/shard_map/all_gather | solution.py:120
  96.1 353.3 %all-gather.17.cloned.1.call-start = ((), (), s32[]{:S(2)}) async-start(), calls=%async_computation.2 | async-start | bytes 1114112 | tf_op jit(solution)/shard_map/all_gather | solution.py:86
  282.2 125.7 %copy-start.1 = (bf16[128,3584]{1,0:T(8,128)(2,1)S(1)}, bf16[128,3584]{1,0:T(8,128)(2,1)}, u32[]{:S(2)}) copy-start(bf16[128,3584]{1,0:T(8,128)(2,1)} %param.13) | copy-start | bytes 2752516
  282.2 126.2 %copy-start.2 = (f32[1,256]{1,0:T(1,128)S(1)}, f32[1,256]{1,0:T(1,128)}, u32[]{:S(2)}) copy-start(f32[1,256]{1,0:T(1,128)} %param.22) | copy-start | bytes 3076
  384.2 23.8 %collective-permute-start = (bf16[128,3584]{1,0:T(8,128)(2,1)}, bf16[128,3584]{1,0:T(8,128)(2,1)S(1)}, u32[]{:S(2)}, u32[]{:S(2)}) collective-permute-start(bf16[128,3584]{1,0:T(8,128)(2,1)} %fusion.29), channel_id=1, source_target_pairs={{0,16},{1,17},{2,18},{3,19},{4,20},{5,21},{6,22},{7,23},{8,24},{9,... | collective-permute-start | bytes 2752520 | tf_op jit(solution)/shard_map/ppermute | solution.py:18
  411.5 7.6 %copy-start.3 = (f32[1,256]{1,0:T(1,128)S(1)}, f32[1,256]{1,0:T(1,128)}, u32[]{:S(2)}) copy-start(f32[1,256]{1,0:T(1,128)} %param.23) | copy-start | bytes 3076
  411.5 75.5 %all-gather.19.cloned.1.call-start = ((), (), s32[]{:S(2)}) async-start(), calls=%async_computation.3 | async-start | bytes 1114112 | tf_op jit(solution)/shard_map/all_gather | solution.py:87
Sparse Core Ops, SparseCore 0:
  10.3 40.6 all-gather.20
  53.2 39.2 all-gather.24
  94.8 100.4 all-gather.22
  198.0 36.9 all-gather.12
  237.5 35.3 all-gather.14
  275.1 101.3 all-gather.26
  411.6 37.7 all-gather.16
  451.5 35.3 all-gather.18
where the time goes:
time: 514 us; the launch traced here: 511 us
  waiting for transfers between devices  391 us (76%)
  matrix products  72.6 us (14%)
  other arithmetic  26.6 us (5%)
  between operations  14.4 us (3%)
    all_gather x1, waiting for transfers between devices, per_device(): lax.all_gather(w_query[0], 'seq', axis=0, tiled=True)  95.5 us
    all_gather x1, waiting for transfers between devices, per_device(): lax.all_gather(w_out[0], 'seq', axis=0, tiled=True)  94.3 us
    all_gather x2, waiting for transfers between devices, attend(): key_piece = lax.all_gather(keys_rot, 'seq', axis=0, tiled=True)  59.6 us
    all_gather x2, waiting for transfers between devices, attend(): value_piece = lax.all_gather(values, 'seq', axis=0, tiled=True)  40.7 us
    all_gather x1, waiting for transfers between devices, per_device(): lax.all_gather(w_value[0], 'seq', axis=0, tiled=True)  38.3 us
    all_gather x1, waiting for transfers between devices, per_device(): lax.all_gather(w_key[0], 'seq', axis=0, tiled=True)  37.9 us
    ppermute x1, waiting for transfers between devices, from_behind(): return lax.ppermute(value, axis, pairs)  22.3 us
    dot_general x2, matrix products, attend(): jnp.einsum('hgqk,khd->hgqd', probs, value_piece, preferred_element_type=j...  18.5 us
  transfers between devices with their start and end apart: 9, of which 9 were waited for; matrix products, arithmetic and copies ran while one was open for 15% of the time, Pallas kernels for 0%

commit v1 on v0

v1 whole, which is shorter than its diff:
```python
import functools
import math

import jax
import jax.numpy as jnp
from jax import lax
from jax.experimental import pallas as pl
from jax.experimental.pallas import tpu as pltpu
from jax.sharding import PartitionSpec as P

HEAD_DIM = 128
HEADS = 14
KV_HEADS = 2
EPSILON = 1e-06
THETA = 1000000.0
MESH = pl.DeviceIdType.MESH

PLANES, CHIPS_X, CORES = 4, 2, 2
CHIPS = PLANES * CHIPS_X


def kernel(
    n_section,
    dims,
    x_ref,
    inc_ref,
    wq_ref,
    wk_ref,
    wv_ref,
    wo_ref,
    gain_ref,
    bias_ref,
    cos_ref,
    sin_ref,
    qcol_ref,
    kcol_ref,
    out1_ref,
    out2_ref,
    wqkv,
    wout,
    xs1,
    xs2,
    hidden,
    acc,
    qs,
    kv1,
    kv2,
    mask,
    ctx1,
    ctx2,
    half1,
    half2,
    loc_sem,
    cx_send,
    cx_recv,
    up_send,
    up_recv,
    dn_send,
    dn_recv,
    xl_send,
    xl_recv,
    kv_send,
    kv_recv,
    ps_send,
    ps_recv,
):
    (rows, d, qw, kvw) = dims
    seq_len = rows * CHIPS * CORES
    tok = rows * CORES
    qh, kh, oh = qw // CORES, kvw // CORES, d // CORES
    group = HEADS // KV_HEADS
    wr, wor = wq_ref.shape[0], wo_ref.shape[0]

    s = lax.axis_index("section")
    me = lax.axis_index("seq")
    chip = me // CORES
    c = me % CORES
    z = chip // CHIPS_X
    x = chip % CHIPS_X
    oc = 1 - c
    ox = 1 - x

    def dev(zz, xx, cc):
        return (s, (zz * CHIPS_X + xx) * CORES + cc)

    partner = dev(z, x, oc)
    x_peer = dev(z, ox, c)
    z_up = dev(jnp.minimum(z + 1, PLANES - 1), x, c)
    z_dn = dev(jnp.maximum(z - 1, 0), x, c)

    sent = []

    def send(src, dst, ssem, rsem, target, cond=None):
        copy = pltpu.make_async_remote_copy(
            src_ref=src, dst_ref=dst, send_sem=ssem, recv_sem=rsem,
            device_id=target, device_id_type=MESH,
        )
        if cond is None:
            copy.start()
        else:
            pl.when(cond)(copy.start)
        sent.append((copy, cond))

    def arrived(ref, rsem, ssem, target):
        pltpu.make_async_remote_copy(
            src_ref=ref, dst_ref=ref, send_sem=ssem, recv_sem=rsem,
            device_id=target, device_id_type=MESH,
        ).wait_recv()

    def at(offset, size, unit=16):
        return pl.ds(pl.multiple_of(offset, unit), size)

    barrier = pltpu.get_barrier_semaphore()

    def greet(target):
        pl.semaphore_signal(barrier, inc=1, device_id=target, device_id_type=MESH)

    greet(partner)
    for step in range(1, CHIPS):
        greet((s, lax.rem(chip + step, CHIPS) * CORES + c))
    has_prev = s > 0
    has_next = s < n_section - 1
    s_prev = (jnp.maximum(s - 1, 0), me)
    s_next = (jnp.minimum(s + 1, n_section - 1), me)
    pl.when(has_prev)(lambda: greet(s_prev))
    pl.when(has_next)(lambda: greet(s_next))
    pl.semaphore_wait(barrier, CHIPS + has_prev.astype(jnp.int32) + has_next.astype(jnp.int32))

    row0 = chip * (CORES * wr) + c * wr
    orow0 = chip * (CORES * wr) + oc * wr
    wrow0 = chip * (CORES * wor) + c * wor
    worow0 = chip * (CORES * wor) + oc * wor
    pieces = [
        (wq_ref, wqkv, row0, orow0, wr, 0, qh),
        (wk_ref, wqkv, row0, orow0, wr, qh, kh),
        (wv_ref, wqkv, row0, orow0, wr, qh + kh, kh),
        (wo_ref, wout, wrow0, worow0, wor, 0, oh),
    ]
    local = []
    for i, (src, dst, r0, _, n, col, width) in enumerate(pieces):
        there = dst.at[at(r0, n), pl.ds(col, width)]
        send(src.at[:, at(oc * width, width, 128)], there, cx_send.at[i], cx_recv.at[i], partner)
        copy = pltpu.make_async_copy(src.at[:, at(c * width, width, 128)], there, loc_sem.at[i])
        copy.start()
        local.append(copy)

    mine = at(c * rows, rows)
    send(x_ref, xs1.at[mine], cx_send.at[4], cx_recv.at[4], partner)
    copy = pltpu.make_async_copy(x_ref, xs1.at[mine], loc_sem.at[4])
    copy.start()
    local.append(copy)
    first = s == 0
    send(inc_ref, xs2.at[mine], cx_send.at[5], cx_recv.at[5], partner, first)
    inc_copy = pltpu.make_async_copy(inc_ref, xs2.at[mine], loc_sem.at[5])
    pl.when(first)(inc_copy.start)

    def own_ready(i):
        _, dst, _, r1, n, col, width = pieces[i]
        local[i].wait()
        arrived(dst.at[at(r1, n), pl.ds(col, width)], cx_recv.at[i], cx_send.at[i], partner)

    bufs = [wqkv, wout]
    shard = [CORES * wr, CORES * wor]
    tails = [80, 32]

    def full(w, zz, xx):
        return bufs[w].at[at((zz * CHIPS_X + xx) * shard[w], shard[w])]

    def apart(w, zz, xx):
        return bufs[w].at[at((zz * CHIPS_X + xx) * shard[w], shard[w] - tails[w])]

    def bpart(w, zz, xx):
        return bufs[w].at[at((zz * CHIPS_X + xx + 1) * shard[w] - tails[w], tails[w])]

    can_up = z < PLANES - 1
    can_dn = z > 0

    def z_send(ref, w, t, part, up, cond):
        ss, rs = (up_send, up_recv) if up else (dn_send, dn_recv)
        target = z_up if up else z_dn
        send(ref, ref, ss.at[w, t, part], rs.at[w, t, part], target, cond)

    def x_send(ref, w, i, cond=None):
        send(ref, ref, xl_send.at[w, i], xl_recv.at[w, i], x_peer, cond)

    def gather_start(w):
        x_send(bpart(w, z, x), w, 0)
        z_send(full(w, z, x), w, 0, 0, True, can_up)
        z_send(full(w, z, x), w, 0, 0, False, can_dn)
        x_send(apart(w, z, x), w, 1)
        other = bpart(w, z, ox)
        arrived(other, xl_recv.at[w, 0], xl_send.at[w, 0], x_peer)
        z_send(other, w, 0, 1, True, can_up)
        z_send(other, w, 0, 1, False, can_dn)

    def gather_step(w, t):
        for up in (True, False):
            zz = z - t if up else z + t
            got = (z >= t) if up else (z + t <= PLANES - 1)
            on = got & (can_up if up else can_dn)
            zc = jnp.clip(zz, 0, PLANES - 1)
            ss, rs = (up_send, up_recv) if up else (dn_send, dn_recv)
            target = z_dn if up else z_up
            for part, ref in ((0, full(w, zc, x)), (1, bpart(w, zc, ox))):
                pl.when(got)(
                    lambda ref=ref, part=part: arrived(
                        ref, rs.at[w, t - 1, part], ss.at[w, t - 1, part], target
                    )
                )
                if t < PLANES - 1:
                    z_send(ref, w, t, part, up, on)
                if part == 0:
                    x_send(apart(w, zc, x), w, (1 if up else PLANES) + t, got)

    def gather_end(w):
        arrived(apart(w, z, ox), xl_recv.at[w, 1], xl_send.at[w, 1], x_peer)
        for t in range(1, PLANES):
            for up in (True, False):
                zz = z - t if up else z + t
                got = (z >= t) if up else (z + t <= PLANES - 1)
                zc = jnp.clip(zz, 0, PLANES - 1)
                i = (1 if up else PLANES) + t
                pl.when(got)(
                    lambda zc=zc, i=i: arrived(
                        apart(w, zc, ox), xl_recv.at[w, i], xl_send.at[w, i], x_peer
                    )
                )

    def norm(src):
        def body(i, carry):
            r = at(i * 32, 32, 32)
            wide = src[r, :].astype(jnp.float32)
            mean = jnp.mean(wide * wide, axis=-1, keepdims=True)
            hidden[r, :] = (wide * lax.rsqrt(mean + EPSILON) * gain_ref[...]).astype(jnp.bfloat16)
            return carry

        lax.fori_loop(0, tok // 32, body, 0)

    def make_mask(p):
        key_col = kcol_ref[p]
        def body(i, carry):
            r = at(i * 32, 32, 32)
            q_col = qcol_ref[p, r, :]
            shape = (32, seq_len)
            qi = chip * tok + i * 32 + lax.broadcasted_iota(jnp.int32, shape, 0)
            ki = lax.broadcasted_iota(jnp.int32, shape, 1)
            ok = (ki <= qi) & ((key_col == q_col) | (key_col == 0))
            mask[r, :] = jnp.where(ok, 0.0, -1e30).astype(jnp.float32)
            return carry

        lax.fori_loop(0, tok // 32, body, 0)

    tile = 3 * HEAD_DIM
    width_all = qh + 2 * kh

    def project(p, kv):
        def body(i, carry):
            cols = at(i * tile, tile, 128)
            acc[:, cols] = (
                jnp.dot(hidden[...], wqkv[:, cols], preferred_element_type=jnp.float32)
                + bias_ref[:, cols]
            )
            return carry

        lax.fori_loop(0, width_all // tile, body, 0)
        cosine, sine = cos_ref[p], sin_ref[p]

        def turn(u):
            return (u * cosine + pltpu.roll(u, HEAD_DIM // 2, 1) * sine).astype(jnp.bfloat16)

        own = at(chip * tok, tok)
        kv[own, pl.ds(0, HEAD_DIM)] = turn(acc[:, pl.ds(qh, HEAD_DIM)])
        kv[own, pl.ds(HEAD_DIM, HEAD_DIM)] = acc[:, pl.ds(qh + kh, HEAD_DIM)].astype(jnp.bfloat16)
        for step in range(1, CHIPS):
            target = (s, lax.rem(chip + step, CHIPS) * CORES + c)
            send(kv.at[own], kv.at[own], kv_send.at[p, step], kv_recv.at[p, step], target)

        def head(h, carry):
            qs[h] = turn(acc[:, at(h * HEAD_DIM, HEAD_DIM, 128)])
            return carry

        lax.fori_loop(0, group, head, 0)

    def keys_ready(p, kv):
        for step in range(1, CHIPS):
            origin = lax.rem(chip + CHIPS - step, CHIPS)
            arrived(
                kv.at[at(origin * tok, tok)], kv_recv.at[p, step], kv_send.at[p, step],
                (s, origin * CORES + c),
            )

    factor = HEAD_DIM ** (-0.5) * math.log2(math.e)

    def attend(kv, ctx, lo, hi):
        def head(h, carry):
            scores = lax.dot_general(
                qs[h], kv[:, pl.ds(0, HEAD_DIM)], (((1,), (1,)), ((), ())),
                preferred_element_type=jnp.float32,
            )
            scores = scores * factor + mask[...]
            probs = jnp.exp2(scores - jnp.max(scores, axis=-1, keepdims=True))
            total = jnp.sum(probs, axis=-1, keepdims=True)
            summed = jnp.dot(
                probs.astype(jnp.bfloat16), kv[:, pl.ds(HEAD_DIM, HEAD_DIM)],
                preferred_element_type=jnp.float32,
            )
            ctx[:, at(c * qh + h * HEAD_DIM, HEAD_DIM, 128)] = (summed / total).astype(jnp.bfloat16)
            return carry

        lax.fori_loop(lo, hi, head, 0)

    def share_ctx(p, ctx):
        ref = ctx.at[:, at(c * qh, qh, 128)]
        send(ref, ref, cx_send.at[6 + p], cx_recv.at[6 + p], partner)

    def ctx_ready(p, ctx):
        arrived(ctx.at[:, at(oc * qh, qh, 128)], cx_recv.at[6 + p], cx_send.at[6 + p], partner)

    def project_out(src, ctx, half):
        def body(i, carry):
            cols = at(i * 256, 256, 256)
            wide = src[:, at(c * oh + i * 256, 256, 256)].astype(jnp.float32)
            half[:, cols] = (
                wide + jnp.dot(ctx[...], wout[:, cols], preferred_element_type=jnp.float32)
            ).astype(jnp.bfloat16)
            return carry

        lax.fori_loop(0, oh // 256, body, 0)

    def give(p, half, out):
        cols = at(c * oh, oh, 128)
        send(
            half.at[at(oc * rows, rows)], out.at[:, cols], cx_send.at[8 + p], cx_recv.at[8 + p],
            partner,
        )
        copy = pltpu.make_async_copy(half.at[mine], out.at[:, cols], loc_sem.at[6 + p])
        copy.start()
        return copy

    def given(p, out):
        arrived(out.at[:, at(oc * oh, oh, 128)], cx_recv.at[8 + p], cx_send.at[8 + p], partner)

    for i in range(3):
        own_ready(i)
    gather_start(0)
    local[4].wait()
    other_rows = at(oc * rows, rows)
    arrived(xs1.at[other_rows], cx_recv.at[4], cx_send.at[4], partner)
    norm(xs1)
    gather_step(0, 1)
    make_mask(0)
    own_ready(3)
    gather_start(1)
    gather_step(0, 2)
    gather_step(0, 3)
    gather_end(0)
    gather_step(1, 1)
    project(0, kv1)
    gather_step(1, 2)
    keys_ready(0, kv1)
    attend(kv1, ctx1, 0, 3)
    gather_step(1, 3)
    attend(kv1, ctx1, 3, group)
    share_ctx(0, ctx1)
    make_mask(1)
    ctx_ready(0, ctx1)
    gather_end(1)
    project_out(xs1, ctx1, half1)

    my_cols = at(c * oh, oh, 128)
    send(half1, xs2.at[:, my_cols], ps_send.at[0], ps_recv.at[0], s_next, has_next)
    out_copy1 = give(0, half1, out1_ref)

    def from_first():
        inc_copy.wait()
        arrived(xs2.at[other_rows], cx_recv.at[5], cx_send.at[5], partner)

    pl.when(first)(from_first)
    cols_ref = xs2.at[:, my_cols]
    pl.when(has_prev)(
        lambda: arrived(cols_ref, ps_recv.at[0], ps_send.at[0], s_prev)
    )
    send(cols_ref, cols_ref, cx_send.at[10], cx_recv.at[10], partner, has_prev)
    pl.when(has_prev)(
        lambda: arrived(
            xs2.at[:, at(oc * oh, oh, 128)], cx_recv.at[10], cx_send.at[10], partner
        )
    )
    norm(xs2)
    project(1, kv2)
    keys_ready(1, kv2)
    attend(kv2, ctx2, 0, group)
    share_ctx(1, ctx2)
    ctx_ready(1, ctx2)
    project_out(xs2, ctx2, half2)
    out_copy2 = give(1, half2, out2_ref)

    given(0, out1_ref)
    given(1, out2_ref)
    out_copy1.wait()
    out_copy2.wait()
    for copy, cond in sent:
        if cond is None:
            copy.wait_send()
        else:
            pl.when(cond)(copy.wait_send)


def per_device(
    n_section,
    activations,
    incoming,
    column_ids,
    positions,
    norm_gain,
    w_query,
    w_key,
    w_value,
    w_out,
    b_query,
    b_key,
    b_value,
):
    _, rows, d = activations.shape
    qw, kvw = w_query.shape[2], w_key.shape[2]
    qh, kh, oh = qw // CORES, kvw // CORES, d // CORES
    tok = rows * CORES
    seq_len = column_ids.shape[1]
    s = lax.axis_index("section")
    me = lax.axis_index("seq")
    chip, core = me // CORES, me % CORES
    second_row = (s + n_section) % (n_section + 1)
    picked = jnp.stack([s, second_row])
    columns = jnp.take(column_ids, picked, axis=0, mode="clip")
    places = jnp.take(positions, picked, axis=0, mode="clip")
    q_cols = lax.dynamic_slice_in_dim(columns, chip * tok, tok, 1)[:, :, None]
    places = lax.dynamic_slice_in_dim(places, chip * tok, tok, 1).astype(jnp.float32)
    half = HEAD_DIM // 2
    freqs = THETA ** (-(jnp.arange(half, dtype=jnp.float32) * 2.0) / HEAD_DIM)
    angles = places[:, :, None] * freqs
    cosine, sine = jnp.cos(angles), jnp.sin(angles)
    cosine = jnp.concatenate([cosine, cosine], axis=-1)
    sine = jnp.concatenate([-sine, sine], axis=-1)
    bias = jnp.concatenate(
        [
            lax.dynamic_slice_in_dim(b_query, core * qh, qh, 1),
            lax.dynamic_slice_in_dim(b_key, core * kh, kh, 1),
            lax.dynamic_slice_in_dim(b_value, core * kh, kh, 1),
        ],
        axis=1,
    )
    bf16, f32 = jnp.bfloat16, jnp.float32
    anywhere = pl.BlockSpec(memory_space=pl.ANY)
    vmem = pl.BlockSpec(memory_space=pltpu.VMEM)
    dma = pltpu.SemaphoreType.DMA
    shape = jax.ShapeDtypeStruct((rows, d), bf16)
    width = qh + 2 * kh
    z_sems = dma((2, PLANES - 1, 2))
    out1, out2 = pl.pallas_call(
        functools.partial(kernel, n_section, (rows, d, qw, kvw)),
        out_shape=(shape, shape),
        in_specs=[anywhere] * 6 + [vmem] * 6,
        out_specs=(anywhere, anywhere),
        scratch_shapes=[
            pltpu.VMEM((d, width), bf16),
            pltpu.VMEM((qw, oh), bf16),
            pltpu.VMEM((tok, d), bf16),
            pltpu.VMEM((tok, d), bf16),
            pltpu.VMEM((tok, d), bf16),
            pltpu.VMEM((tok, width), f32),
            pltpu.VMEM((HEADS // KV_HEADS, tok, HEAD_DIM), bf16),
            pltpu.VMEM((seq_len, 2 * HEAD_DIM), bf16),
            pltpu.VMEM((seq_len, 2 * HEAD_DIM), bf16),
            pltpu.VMEM((tok, seq_len), f32),
            pltpu.VMEM((tok, qw), bf16),
            pltpu.VMEM((tok, qw), bf16),
            pltpu.VMEM((tok, oh), bf16),
            pltpu.VMEM((tok, oh), bf16),
            dma((8,)),
            dma((11,)),
            dma((11,)),
            z_sems,
            z_sems,
            z_sems,
            z_sems,
            dma((2, 2 * PLANES)),
            dma((2, 2 * PLANES)),
            dma((2, CHIPS)),
            dma((2, CHIPS)),
            dma((1,)),
            dma((1,)),
        ],
        compiler_params=pltpu.CompilerParams(
            collective_id=0, has_side_effects=True, vmem_limit_bytes=56 * 1024 * 1024
        ),
        name="two_sections",
    )(
        activations[0],
        incoming,
        w_query[0],
        w_key[0],
        w_value[0],
        w_out[0],
        norm_gain,
        bias,
        cosine,
        sine,
        q_cols,
        columns[:, None, :],
    )
    return (out1[None], out2[None])


def solution(mesh):
    placed = (
        P("section", "seq", None),
        P("seq", None),
        P(),
        P(),
        P("section", None),
        P("section", "seq", None),
        P("section", "seq", None),
        P("section", "seq", None),
        P("section", "seq", None),
        P("section", None),
        P("section", None),
        P("section", None),
    )
    return jax.shard_map(
        functools.partial(per_device, mesh.shape["section"]),
        mesh=mesh,
        in_specs=placed,
        out_specs=(P("section", "seq", None), P("section", "seq", None)),
        check_vma=False,
    )
```

time: 514 us -> 259 us (0.50)
  waiting for transfers between devices: 391 us -> 0 us
  Pallas kernels: 0 us -> 247 us
  matrix products: 72.6 us -> 0 us
  other arithmetic: 26.6 us -> 2.69 us
  between operations: 14.4 us -> 0.75 us
    all_gather x8 -> x0, waiting for transfers between devices: 366 us -> none  [the longest x1 95.5 us: per_device(): lax.all_gather(w_query[0], 'seq', axis=0, tiled=True)]
    pallas_call x0 -> x1, Pallas kernels: none -> 247 us  [per_device(): pl.pallas_call(functools.partial(kernel, n_section, (rows, d, qw, kvw)),...]
    dot_general x12 -> x0, matrix products: 72.6 us -> none  [the longest x2 18.5 us: attend(): jnp.einsum('hgqk,khd->hgqd', probs, value_piece, preferred_element_type=j...]
    ppermute x1 -> x0, waiting for transfers between devices: 22.3 us -> none  [from_behind(): return lax.ppermute(value, axis, pairs)]
    reduce_sum x4 -> x0, other arithmetic: 19.1 us -> none  [the longest x2 17.3 us: attend(): total = jnp.sum(exponentials, axis=-1)]
  transfers between devices with their start and end apart: 9 -> 0, of which waited for: 9 -> 0; matrix products, arithmetic and copies ran while one was open for 15% -> 0% of each run, Pallas kernels for 0% -> 0%
where the time goes in v1:
time: 259 us; the launch traced here: 257 us
  Pallas kernels  247 us (95%)
  local copies, waits for them, and re-layouts  6.63 us (3%)
  other arithmetic  2.69 us (1%)
    pallas_call x1, Pallas kernels, per_device(): pl.pallas_call(functools.partial(kernel, n_section, (rows, d, qw, kvw)),...  247 us

profile of v1, /device:TPU:29, one launch (start us, length us, event | category | flops | bytes accessed | tf_op | source)
XLA Modules:
  0.0 256.8 jit_solution(703311926888384748)
XLA Ops:
  0.6 0.0 copy-start
  0.7 0.1 pad_add_fusion
  0.8 0.0 copy-start.4
  0.8 0.0 copy-start.5
  0.8 0.0 copy-start.3
  0.8 0.7 copy-done.4
  1.5 0.0 copy-done.5
  1.5 0.0 copy-done.3
  1.5 0.6 pad_maximum_fusion.2.bias_ref
  2.1 0.0 copy-done
  2.1 0.6 gather_fusion.1
  2.7 0.0 copy-start.2
  2.7 0.6 broadcast_in_dim.21.kcol_ref
  3.3 0.1 copy-done.2
  3.4 0.6 gather_fusion
  4.0 0.9 copy.14.qcol_ref
  4.9 1.0 fusion
  5.9 1.0 pad_maximum_fusion
  6.9 246.8 %two_sections.1 = (bf16[128,3584]{1,0:T(8,128)(2,1)}, bf16[128,3584]{1,0:T(8,128)(2,1)}) custom-call(bf16[128,3584]{1,0:T(8,128)(2,1)} %bitcast.13, bf16[128,3584]{1,0:T(8,128)(2,1)} %inc_ref.1, bf16[224,1792]{1,0:T(8,128)(2,1)} %bitcast.14, bf16[224,256]{1,0:T(8,128)(2,1)} %bitcast.16, bf16[224,256]{1,0:T(8,128)(2,1)} %bitcast.17, ...), custom_call_target="tpu_custom_call" | custom-call | tf_op jit(solution)/shard_map/two_sections/pallas_call | solution.py:459
  253.7 0.0 copy-start.1
  253.7 2.2 copy.17
  255.9 0.0 copy-done.1
  255.9 0.9 copy.18
  (6 shorter events, 0.0 us)
Async XLA Ops:
  0.6 1.5 copy-start
  0.8 0.7 copy-start.4
  0.8 0.7 copy-start.5
  0.8 0.7 copy-start.3
  2.7 0.8 copy-start.2
  253.7 2.3 copy-start.1

commit v2 on v1

v2 whole, which is shorter than its diff:
```python
import functools
import math

import jax
import jax.numpy as jnp
from jax import lax
from jax.experimental import pallas as pl
from jax.experimental.pallas import tpu as pltpu
from jax.sharding import PartitionSpec as P

HEAD_DIM = 128
HEADS = 14
KV_HEADS = 2
EPSILON = 1e-06
THETA = 1000000.0
MESH = pl.DeviceIdType.MESH

PLANES, CHIPS_X, CORES = 4, 2, 2
CHIPS = PLANES * CHIPS_X


def kernel(
    n_section,
    dims,
    x_ref,
    inc_ref,
    wq_ref,
    wk_ref,
    wv_ref,
    wo_ref,
    gain_ref,
    bq_ref,
    bk_ref,
    bv_ref,
    freq_ref,
    cols_ref,
    pos_ref,
    out1_ref,
    out2_ref,
    wqkv,
    wout_a,
    wout_b,
    wout_c,
    xs1,
    xs2,
    hidden,
    acc,
    squares,
    turns,
    q_cols,
    qs,
    kv1,
    kv2,
    mask,
    ctx1,
    ctx2,
    half1,
    half2,
    loc_sem,
    cx_send,
    cx_recv,
    up_send,
    up_recv,
    dn_send,
    dn_recv,
    xl_send,
    xl_recv,
    kv_send,
    kv_recv,
    ps_send,
    ps_recv,
):
    (rows, d, qw, kvw) = dims
    seq_len = rows * CHIPS * CORES
    tok = rows * CORES
    qh, kh, oh = qw // CORES, kvw // CORES, d // CORES
    group = HEADS // KV_HEADS
    wr, wor = wq_ref.shape[0], wo_ref.shape[0]

    s = lax.axis_index("section")
    me = lax.axis_index("seq")
    chip = me // CORES
    c = me % CORES
    z = chip // CHIPS_X
    x = chip % CHIPS_X
    oc = 1 - c
    ox = 1 - x

    def dev(zz, xx, cc):
        return (s, (zz * CHIPS_X + xx) * CORES + cc)

    partner = dev(z, x, oc)
    x_peer = dev(z, ox, c)
    z_up = dev(jnp.minimum(z + 1, PLANES - 1), x, c)
    z_dn = dev(jnp.maximum(z - 1, 0), x, c)

    sent = []

    def send(src, dst, ssem, rsem, target, cond=None):
        copy = pltpu.make_async_remote_copy(
            src_ref=src, dst_ref=dst, send_sem=ssem, recv_sem=rsem,
            device_id=target, device_id_type=MESH,
        )
        if cond is None:
            copy.start()
        else:
            pl.when(cond)(copy.start)
        sent.append((copy, cond))

    def arrived(ref, rsem, ssem, target):
        pltpu.make_async_remote_copy(
            src_ref=ref, dst_ref=ref, send_sem=ssem, recv_sem=rsem,
            device_id=target, device_id_type=MESH,
        ).wait_recv()

    def at(offset, size, unit=16):
        return pl.ds(pl.multiple_of(offset, unit), size)

    kv1[...] = jnp.zeros_like(kv1)
    kv2[...] = jnp.zeros_like(kv2)

    barrier = pltpu.get_barrier_semaphore()

    def greet(target):
        pl.semaphore_signal(barrier, inc=1, device_id=target, device_id_type=MESH)

    greet(partner)
    greet(x_peer)
    can_up = z < PLANES - 1
    can_dn = z > 0
    pl.when(can_up)(lambda: greet(z_up))
    pl.when(can_dn)(lambda: greet(z_dn))
    has_prev = s > 0
    has_next = s < n_section - 1
    s_prev = (jnp.maximum(s - 1, 0), me)
    s_next = (jnp.minimum(s + 1, n_section - 1), me)
    pl.when(has_prev)(lambda: greet(s_prev))
    pl.when(has_next)(lambda: greet(s_next))
    peers = 2
    for there in (can_up, can_dn, has_prev, has_next):
        peers = peers + there.astype(jnp.int32)
    pl.semaphore_wait(barrier, peers)

    row0 = chip * (CORES * wr) + c * wr
    orow0 = chip * (CORES * wr) + oc * wr
    wrow0 = chip * (CORES * wor) + c * wor
    worow0 = chip * (CORES * wor) + oc * wor
    wouts = [wout_a, wout_b, wout_c]
    chunks = []
    low = 0
    for buf in wouts:
        chunks.append((low, buf.shape[1]))
        low += buf.shape[1]
    pieces = [
        (wq_ref, wqkv, row0, orow0, wr, qh, 0, 0),
        (wk_ref, wqkv, row0, orow0, wr, kh, 0, qh),
        (wv_ref, wqkv, row0, orow0, wr, kh, 0, qh + kh),
    ] + [
        (wo_ref, buf, wrow0, worow0, wor, oh, lo, 0) for buf, (lo, _) in zip(wouts, chunks)
    ]
    widths = [qh, kh, kh] + [w for _, w in chunks]
    local = []
    for i, (src, dst, r0, _, n, part, lo, col) in enumerate(pieces):
        width = widths[i]
        there = dst.at[at(r0, n), pl.ds(col, width)]
        send(
            src.at[:, at(oc * part + lo, width, 128)], there, cx_send.at[i], cx_recv.at[i], partner
        )
        copy = pltpu.make_async_copy(
            src.at[:, at(c * part + lo, width, 128)], there, loc_sem.at[i]
        )
        copy.start()
        local.append(copy)

    mine = at(c * rows, rows)
    send(x_ref, xs1.at[mine], cx_send.at[6], cx_recv.at[6], partner)
    copy = pltpu.make_async_copy(x_ref, xs1.at[mine], loc_sem.at[6])
    copy.start()
    local.append(copy)
    first = s == 0
    send(inc_ref, xs2.at[mine], cx_send.at[7], cx_recv.at[7], partner, first)
    inc_copy = pltpu.make_async_copy(inc_ref, xs2.at[mine], loc_sem.at[7])
    pl.when(first)(inc_copy.start)

    def own_ready(i):
        _, dst, _, r1, n, _, _, col = pieces[i]
        local[i].wait()
        arrived(dst.at[at(r1, n), pl.ds(col, widths[i])], cx_recv.at[i], cx_send.at[i], partner)

    bufs = [wqkv] + wouts
    shard = [CORES * wr] + [CORES * wor] * len(wouts)
    tails = [80] + [32] * len(wouts)

    def apart(w, zz, xx):
        return bufs[w].at[at((zz * CHIPS_X + xx) * shard[w], shard[w] - tails[w])]

    def bpart(w, zz, xx):
        return bufs[w].at[at((zz * CHIPS_X + xx + 1) * shard[w] - tails[w], tails[w])]

    def z_send(ref, w, t, part, up, cond):
        ss, rs = (up_send, up_recv) if up else (dn_send, dn_recv)
        target = z_up if up else z_dn
        send(ref, ref, ss.at[w, t, part], rs.at[w, t, part], target, cond)

    def x_send(ref, w, i, cond=None):
        send(ref, ref, xl_send.at[w, i], xl_recv.at[w, i], x_peer, cond)

    def flow(up, t):
        zz = z - t if up else z + t
        got = (z >= t) if up else (z + t <= PLANES - 1)
        on = got & (can_up if up else can_dn)
        return jnp.clip(zz, 0, PLANES - 1), got, on

    def a_start(w):
        x_send(bpart(w, z, x), w, 0)
        z_send(apart(w, z, x), w, 0, 0, True, can_up)
        z_send(apart(w, z, x), w, 0, 0, False, can_dn)
        x_send(apart(w, z, x), w, 1)

    def b_start(w):
        other = bpart(w, z, ox)
        arrived(other, xl_recv.at[w, 0], xl_send.at[w, 0], x_peer)
        for part, ref in ((1, bpart(w, z, x)), (2, other)):
            z_send(ref, w, 0, part, True, can_up)
            z_send(ref, w, 0, part, False, can_dn)

    def z_arrived(ref, w, t, part, up, got):
        ss, rs = (up_send, up_recv) if up else (dn_send, dn_recv)
        target = z_dn if up else z_up
        pl.when(got)(
            lambda: arrived(ref, rs.at[w, t - 1, part], ss.at[w, t - 1, part], target)
        )

    def a_step(w, t):
        for up in (True, False):
            zc, got, on = flow(up, t)
            ref = apart(w, zc, x)
            z_arrived(ref, w, t, 0, up, got)
            if t < PLANES - 1:
                z_send(ref, w, t, 0, up, on)
            x_send(ref, w, (1 if up else PLANES) + t, got)

    def b_step(w, t):
        for up in (True, False):
            zc, got, on = flow(up, t)
            for part, ref in ((1, bpart(w, zc, x)), (2, bpart(w, zc, ox))):
                z_arrived(ref, w, t, part, up, got)
                if t < PLANES - 1:
                    z_send(ref, w, t, part, up, on)

    def b_steps(w):
        for t in range(1, PLANES):
            b_step(w, t)

    def gather_end(w):
        arrived(apart(w, z, ox), xl_recv.at[w, 1], xl_send.at[w, 1], x_peer)
        for t in range(1, PLANES):
            for up in (True, False):
                zc, got, _ = flow(up, t)
                i = (1 if up else PLANES) + t
                pl.when(got)(
                    lambda zc=zc, i=i: arrived(
                        apart(w, zc, ox), xl_recv.at[w, i], xl_send.at[w, i], x_peer
                    )
                )

    micro = [s, lax.rem(s + n_section, n_section + 1)]

    def tables(p):
        own = at(chip * tok, tok, 128)
        eye = lax.broadcasted_iota(jnp.int32, (tok, tok), 0) == lax.broadcasted_iota(
            jnp.int32, (tok, tok), 1
        )

        def upright(ref):
            entries = ref[pl.ds(micro[p], 1), own].astype(jnp.float32)
            return jnp.sum(jnp.where(eye, entries, 0.0), axis=1, keepdims=True)

        q_cols[p] = jnp.broadcast_to(upright(cols_ref), (tok, HEAD_DIM))
        angles = upright(pos_ref) * freq_ref[0:1, :]
        turns[p, 0] = jnp.cos(angles)
        turns[p, 1] = jnp.sin(angles) * freq_ref[1:2, :]

    def make_mask(p):
        key_col = cols_ref[pl.ds(micro[p], 1), :].astype(jnp.float32)

        def body(i, carry):
            r = at(i * 32, 32, 32)
            q_col = q_cols[p, r, 0:1]
            shape = (32, seq_len)
            qi = chip * tok + i * 32 + lax.broadcasted_iota(jnp.int32, shape, 0)
            ki = lax.broadcasted_iota(jnp.int32, shape, 1)
            ok = (ki <= qi) & ((key_col == q_col) | (key_col == 0.0))
            mask[r, :] = jnp.where(ok, 0.0, -1e30).astype(jnp.float32)
            return carry

        lax.fori_loop(0, tok // 32, body, 0)

    def scale_in(src, lo, width, start):
        def body(i, carry):
            r = at(i * 32, 32, 32)
            total = jnp.zeros((32, 1), jnp.float32)
            for cc in range(CORES):
                cols = pl.ds(cc * oh + lo, width)
                wide = src[r, cols].astype(jnp.float32)
                hidden[r, cols] = (wide * gain_ref[:, cols]).astype(jnp.bfloat16)
                total += jnp.sum(wide * wide, axis=-1, keepdims=True)
            total = jnp.broadcast_to(total, (32, HEAD_DIM))
            squares[r, :] = total if start else squares[r, :] + total
            return carry

        lax.fori_loop(0, tok // 32, body, 0)

    def multiply(lo, width, col, n, start):
        total = 0.0
        for cc in range(CORES):
            part = pl.ds(cc * oh + lo, width)
            total += jnp.dot(
                hidden[:, part], wqkv[part, pl.ds(col, n)], preferred_element_type=jnp.float32
            )
        cols = pl.ds(col, n)
        acc[:, cols] = total if start else acc[:, cols] + total

    def row_factor():
        return lax.rsqrt(squares[...] * (1.0 / d) + EPSILON)

    def turn(p, u):
        return (u * turns[p, 0] + pltpu.roll(u, HEAD_DIM // 2, 1) * turns[p, 1]).astype(
            jnp.bfloat16
        )

    def kv_rows(kv, zz, xx):
        return kv.at[at((zz * CHIPS_X + xx) * tok, tok)]

    def kv_x_send(p, ref, i, cond):
        send(ref, ref, kv_send.at[p, 1, i], kv_recv.at[p, 1, i], x_peer, cond)

    def kv_z_send(p, ref, i, cond):
        send(ref, ref, kv_send.at[p, 0, i], kv_recv.at[p, 0, i], z_up, cond)

    def finish_keys(p, kv):
        factor = row_factor()
        own = at(chip * tok, tok)
        key_bias = bk_ref[:, at(c * kh, kh, 128)]
        value_bias = bv_ref[:, at(c * kh, kh, 128)]
        kv[own, pl.ds(0, kh)] = turn(p, acc[:, pl.ds(qh, kh)] * factor + key_bias)
        kv[own, pl.ds(kh, kh)] = (acc[:, pl.ds(qh + kh, kh)] * factor + value_bias).astype(
            jnp.bfloat16
        )
        mine_kv = kv_rows(kv, z, x)
        kv_z_send(p, mine_kv, 0, can_up)
        kv_x_send(p, mine_kv, 0, x < ox)

    def finish_queries(p):
        factor = row_factor()

        def head(h, carry):
            cols = at(h * HEAD_DIM, HEAD_DIM, 128)
            query_bias = bq_ref[:, at(c * qh + h * HEAD_DIM, HEAD_DIM, 128)]
            qs[h] = turn(p, acc[:, cols] * factor + query_bias)
            return carry

        lax.fori_loop(0, group, head, 0)

    def kv_step(p, kv, t):
        zc, got, on = flow(True, t)
        ref = kv_rows(kv, zc, x)
        pl.when(got)(
            lambda: arrived(ref, kv_recv.at[p, 0, t - 1], kv_send.at[p, 0, t - 1], z_dn)
        )
        if t < PLANES - 1:
            kv_z_send(p, ref, t, on)
        kv_x_send(p, ref, t, got)

    def keys_ready(p, kv):
        for t in range(PLANES):
            zc, got, _ = flow(True, t)
            pl.when(got if t else x > ox)(
                lambda zc=zc, t=t: arrived(
                    kv_rows(kv, zc, ox), kv_recv.at[p, 1, t], kv_send.at[p, 1, t], x_peer
                )
            )

    exp_factor = HEAD_DIM ** (-0.5) * math.log2(math.e)

    def attend(kv, ctx, lo, hi):
        def head(h, carry):
            scores = lax.dot_general(
                qs[h], kv[:, pl.ds(0, HEAD_DIM)], (((1,), (1,)), ((), ())),
                preferred_element_type=jnp.float32,
            )
            scores = scores * exp_factor + mask[...]
            probs = jnp.exp2(scores - jnp.max(scores, axis=-1, keepdims=True))
            total = jnp.sum(probs, axis=-1, keepdims=True)
            summed = jnp.dot(
                probs.astype(jnp.bfloat16), kv[:, pl.ds(HEAD_DIM, HEAD_DIM)],
                preferred_element_type=jnp.float32,
            )
            ctx[:, at(c * qh + h * HEAD_DIM, HEAD_DIM, 128)] = (summed / total).astype(jnp.bfloat16)
            return carry

        lax.fori_loop(lo, hi, head, 0)

    def share_ctx(p, ctx):
        ref = ctx.at[:, at(c * qh, qh, 128)]
        send(ref, ref, cx_send.at[8 + p], cx_recv.at[8 + p], partner)

    def ctx_ready(p, ctx):
        arrived(ctx.at[:, at(oc * qh, qh, 128)], cx_recv.at[8 + p], cx_send.at[8 + p], partner)

    def project_out(src, ctx, half, j):
        lo, width = chunks[j]
        wide = src[:, at(c * oh + lo, width, 128)].astype(jnp.float32)
        half[:, pl.ds(lo, width)] = (
            wide + jnp.dot(ctx[...], wouts[j][...], preferred_element_type=jnp.float32)
        ).astype(jnp.bfloat16)

    def give(p, half, out):
        cols = at(c * oh, oh, 128)
        send(
            half.at[at(oc * rows, rows)], out.at[:, cols], cx_send.at[10 + p], cx_recv.at[10 + p],
            partner,
        )
        copy = pltpu.make_async_copy(half.at[mine], out.at[:, cols], loc_sem.at[8 + p])
        copy.start()
        return copy

    def given(p, out):
        arrived(out.at[:, at(oc * oh, oh, 128)], cx_recv.at[10 + p], cx_send.at[10 + p], partner)

    def pass_on(j):
        lo, width = chunks[j]
        send(
            half1.at[:, pl.ds(lo, width)], xs2.at[:, at(c * oh + lo, width, 128)],
            ps_send.at[j], ps_recv.at[j], s_next, has_next,
        )

    def passed(j):
        lo, width = chunks[j]
        ref = xs2.at[:, at(c * oh + lo, width, 128)]
        pl.when(has_prev)(lambda: arrived(ref, ps_recv.at[j], ps_send.at[j], s_prev))
        send(ref, ref, cx_send.at[12 + j], cx_recv.at[12 + j], partner, has_prev)
        pl.when(has_prev)(
            lambda: arrived(
                xs2.at[:, at(oc * oh + lo, width, 128)], cx_recv.at[12 + j], cx_send.at[12 + j],
                partner,
            )
        )
        scale_in(xs2, lo, width, j == 0)

    for i in range(3):
        own_ready(i)
    a_start(0)
    tables(0)
    tables(1)
    make_mask(0)
    local[6].wait()
    other_rows = at(oc * rows, rows)
    arrived(xs1.at[other_rows], cx_recv.at[6], cx_send.at[6], partner)
    scale_in(xs1, 0, oh, True)
    for i in range(3, len(pieces)):
        own_ready(i)

    def from_first():
        inc_copy.wait()
        arrived(xs2.at[other_rows], cx_recv.at[7], cx_send.at[7], partner)

    pl.when(first)(from_first)
    a_step(0, 1)
    a_step(0, 2)
    a_start(1)
    a_step(0, 3)
    b_start(0)
    b_steps(0)
    a_step(1, 1)
    gather_end(0)
    multiply(0, oh, qh, 2 * kh, True)
    finish_keys(0, kv1)
    multiply(0, oh, 0, qh, True)
    finish_queries(0)
    a_step(1, 2)
    a_start(2)
    a_step(1, 3)
    b_start(1)
    b_steps(1)
    for t in range(1, PLANES):
        kv_step(0, kv1, t)
    a_step(2, 1)
    keys_ready(0, kv1)
    attend(kv1, ctx1, 0, 3)
    a_step(2, 2)
    a_start(3)
    attend(kv1, ctx1, 3, group)
    share_ctx(0, ctx1)
    a_step(2, 3)
    b_start(2)
    b_steps(2)
    a_step(3, 1)
    make_mask(1)
    ctx_ready(0, ctx1)
    gather_end(1)
    project_out(xs1, ctx1, half1, 0)
    pass_on(0)
    a_step(3, 2)
    a_step(3, 3)
    b_start(3)
    gather_end(2)
    project_out(xs1, ctx1, half1, 1)
    pass_on(1)
    passed(0)
    multiply(*chunks[0], qh, 2 * kh, True)
    multiply(*chunks[0], 0, qh, True)
    b_steps(3)
    passed(1)
    multiply(*chunks[1], qh, 2 * kh, False)
    multiply(*chunks[1], 0, qh, False)
    gather_end(3)
    project_out(xs1, ctx1, half1, 2)
    pass_on(2)
    out_copy1 = give(0, half1, out1_ref)
    passed(2)
    multiply(*chunks[2], qh, 2 * kh, False)
    finish_keys(1, kv2)
    multiply(*chunks[2], 0, qh, False)
    finish_queries(1)
    for t in range(1, PLANES):
        kv_step(1, kv2, t)
    keys_ready(1, kv2)
    attend(kv2, ctx2, 0, group)
    share_ctx(1, ctx2)
    ctx_ready(1, ctx2)
    for j in range(len(chunks)):
        project_out(xs2, ctx2, half2, j)
    out_copy2 = give(1, half2, out2_ref)

    given(0, out1_ref)
    given(1, out2_ref)
    out_copy1.wait()
    out_copy2.wait()
    for copy, cond in sent:
        if cond is None:
            copy.wait_send()
        else:
            pl.when(cond)(copy.wait_send)


def per_device(
    n_section,
    activations,
    incoming,
    column_ids,
    positions,
    norm_gain,
    w_query,
    w_key,
    w_value,
    w_out,
    b_query,
    b_key,
    b_value,
):
    _, rows, d = activations.shape
    qw, kvw = w_query.shape[2], w_key.shape[2]
    qh, kh, oh = qw // CORES, kvw // CORES, d // CORES
    tok = rows * CORES
    seq_len = column_ids.shape[1]
    half = HEAD_DIM // 2
    freqs = THETA ** (-(jnp.arange(half, dtype=jnp.float32) * 2.0) / HEAD_DIM)
    signs = jnp.ones((half,), jnp.float32)
    freqs = jnp.stack([jnp.concatenate([freqs, freqs]), jnp.concatenate([-signs, signs])])
    cuts = [oh * 3 // 7, oh * 5 // 14, oh * 3 // 14]
    bf16, f32 = jnp.bfloat16, jnp.float32
    anywhere = pl.BlockSpec(memory_space=pl.ANY)
    vmem = pl.BlockSpec(memory_space=pltpu.VMEM)
    dma = pltpu.SemaphoreType.DMA
    shape = jax.ShapeDtypeStruct((rows, d), bf16)
    width = qh + 2 * kh
    jobs = 1 + len(cuts)
    z_sems = dma((jobs, PLANES - 1, 3))
    out1, out2 = pl.pallas_call(
        functools.partial(kernel, n_section, (rows, d, qw, kvw)),
        out_shape=(shape, shape),
        in_specs=[anywhere] * 6 + [vmem] * 7,
        out_specs=(anywhere, anywhere),
        scratch_shapes=[
            pltpu.VMEM((d, width), bf16),
            *[pltpu.VMEM((qw, cut), bf16) for cut in cuts],
            pltpu.VMEM((tok, d), bf16),
            pltpu.VMEM((tok, d), bf16),
            pltpu.VMEM((tok, d), bf16),
            pltpu.VMEM((tok, width), f32),
            pltpu.VMEM((tok, HEAD_DIM), f32),
            pltpu.VMEM((2, 2, tok, HEAD_DIM), f32),
            pltpu.VMEM((2, tok, HEAD_DIM), f32),
            pltpu.VMEM((HEADS // KV_HEADS, tok, HEAD_DIM), bf16),
            pltpu.VMEM((seq_len, 2 * HEAD_DIM), bf16),
            pltpu.VMEM((seq_len, 2 * HEAD_DIM), bf16),
            pltpu.VMEM((tok, seq_len), f32),
            pltpu.VMEM((tok, qw), bf16),
            pltpu.VMEM((tok, qw), bf16),
            pltpu.VMEM((tok, oh), bf16),
            pltpu.VMEM((tok, oh), bf16),
            dma((10,)),
            dma((15,)),
            dma((15,)),
            z_sems,
            z_sems,
            z_sems,
            z_sems,
            dma((jobs, 2 * PLANES)),
            dma((jobs, 2 * PLANES)),
            dma((2, 2, PLANES)),
            dma((2, 2, PLANES)),
            dma((len(cuts),)),
            dma((len(cuts),)),
        ],
        compiler_params=pltpu.CompilerParams(
            collective_id=0, has_side_effects=True, vmem_limit_bytes=56 * 1024 * 1024
        ),
        name="two_sections",
    )(
        activations[0],
        incoming,
        w_query[0],
        w_key[0],
        w_value[0],
        w_out[0],
        norm_gain,
        b_query,
        b_key,
        b_value,
        freqs,
        column_ids,
        positions,
    )
    return (out1[None], out2[None])


def solution(mesh):
    placed = (
        P("section", "seq", None),
        P("seq", None),
        P(),
        P(),
        P("section", None),
        P("section", "seq", None),
        P("section", "seq", None),
        P("section", "seq", None),
        P("section", "seq", None),
        P("section", None),
        P("section", None),
        P("section", None),
    )
    return jax.shard_map(
        functools.partial(per_device, mesh.shape["section"]),
        mesh=mesh,
        in_specs=placed,
        out_specs=(P("section", "seq", None), P("section", "seq", None)),
        check_vma=False,
    )
```

time: 259 us -> 211 us (0.81)
  Pallas kernels: 247 us -> 206 us
  local copies, waits for them, and re-layouts: 6.63 us -> 3.74 us
    pallas_call x1, Pallas kernels: 247 us -> 206 us  [per_device(): pl.pallas_call(functools.partial(kernel, n_section, (rows, d, qw, kvw)),...]
where the time goes in v2:
time: 211 us
  Pallas kernels  206 us (98%)
  local copies, waits for them, and re-layouts  3.74 us (2%)
    pallas_call x1, Pallas kernels, per_device(): pl.pallas_call(functools.partial(kernel, n_section, (rows, d, qw, kvw)),...  206 us

profile of v2, /device:TPU:29, one launch (start us, length us, event | category | flops | bytes accessed | tf_op | source)
XLA Modules:
  0.0 211.0 jit_solution(15047693569994941327)
XLA Ops:
  0.6 0.0 copy-start.1
  0.7 0.1 maximum_bitcast_fusion
  0.7 0.6 copy-done.1
  1.3 0.6 pad_maximum_fusion.freq_ref
  1.9 205.9 %two_sections.1 = (bf16[128,3584]{1,0:T(8,128)(2,1)}, bf16[128,3584]{1,0:T(8,128)(2,1)}) custom-call(bf16[128,3584]{1,0:T(8,128)(2,1)} %bitcast.9, bf16[128,3584]{1,0:T(8,128)(2,1)} %inc_ref.1, bf16[224,1792]{1,0:T(8,128)(2,1)} %bitcast.12, bf16[224,256]{1,0:T(8,128)(2,1)} %bitcast.14, bf16[224,256]{1,0:T(8,128)(2,1)} %bitcast.15, ...), custom_call_target="tpu_custom_call" | custom-call | tf_op jit(solution)/shard_map/two_sections/pallas_call | solution.py:580
  207.8 0.0 copy-start
  207.8 2.2 %copy.16 = bf16[1,128,3584]{2,1,0:T(8,128)(2,1)} copy(bf16[1,128,3584]{2,1,0:T(8,128)(2,1)} %bitcast.11) | data formatting | bytes 1835008
  210.1 0.0 copy-done
  210.1 0.9 copy.17
  (1 shorter events, 0.0 us)
Async XLA Ops:
  0.6 0.7 copy-start.1
  207.8 2.3 %copy-start = (bf16[128,3584]{1,0:T(8,128)(2,1)S(1)}, bf16[128,3584]{1,0:T(8,128)(2,1)}, u32[]{:S(2)}) copy-start(bf16[128,3584]{1,0:T(8,128)(2,1)} %get-tuple-element.5) | copy-start | bytes 2752516

commit v3 on v2

--- a/solution.py
+++ b/solution.py
@@ -49,6 +49,9 @@
     turns,
     q_cols,
     qs,
+    tops,
+    sums,
+    mixed,
     kv1,
     kv2,
     mask,
@@ -56,6 +59,7 @@
     ctx2,
     half1,
     half2,
+    partial,
     loc_sem,
     cx_send,
     cx_recv,
@@ -264,6 +268,7 @@
                     )
                 )
 
+    exp_factor = HEAD_DIM ** (-0.5) * math.log2(math.e)
     micro = [s, lax.rem(s + n_section, n_section + 1)]
 
     def tables(p):
@@ -325,9 +330,7 @@
         return lax.rsqrt(squares[...] * (1.0 / d) + EPSILON)
 
     def turn(p, u):
-        return (u * turns[p, 0] + pltpu.roll(u, HEAD_DIM // 2, 1) * turns[p, 1]).astype(
-            jnp.bfloat16
-        )
+        return u * turns[p, 0] + pltpu.roll(u, HEAD_DIM // 2, 1) * turns[p, 1]
 
     def kv_rows(kv, zz, xx):
         return kv.at[at((zz * CHIPS_X + xx) * tok, tok)]
@@ -343,7 +346,9 @@
         own = at(chip * tok, tok)
         key_bias = bk_ref[:, at(c * kh, kh, 128)]
         value_bias = bv_ref[:, at(c * kh, kh, 128)]
-        kv[own, pl.ds(0, kh)] = turn(p, acc[:, pl.ds(qh, kh)] * factor + key_bias)
+        kv[own, pl.ds(0, kh)] = turn(p, acc[:, pl.ds(qh, kh)] * factor + key_bias).astype(
+            jnp.bfloat16
+        )
         kv[own, pl.ds(kh, kh)] = (acc[:, pl.ds(qh + kh, kh)] * factor + value_bias).astype(
             jnp.bfloat16
         )
@@ -357,7 +362,8 @@
         def head(h, carry):
             cols = at(h * HEAD_DIM, HEAD_DIM, 128)
             query_bias = bq_ref[:, at(c * qh + h * HEAD_DIM, HEAD_DIM, 128)]
-            qs[h] = turn(p, acc[:, cols] * factor + query_bias)
+            turned = turn(p, acc[:, cols] * factor + query_bias)
+            qs[h] = (turned * exp_factor).astype(jnp.bfloat16)
             return carry
 
         lax.fori_loop(0, group, head, 0)
@@ -372,34 +378,57 @@
             kv_z_send(p, ref, t, on)
         kv_x_send(p, ref, t, got)
 
-    def keys_ready(p, kv):
-        for t in range(PLANES):
-            zc, got, _ = flow(True, t)
-            pl.when(got if t else x > ox)(
-                lambda zc=zc, t=t: arrived(
-                    kv_rows(kv, zc, ox), kv_recv.at[p, 1, t], kv_send.at[p, 1, t], x_peer
-                )
-            )
-
-    exp_factor = HEAD_DIM ** (-0.5) * math.log2(math.e)
-
-    def attend(kv, ctx, lo, hi):
+    plane = CHIPS_X * tok
+
+    def attend(p, kv, t):
+        zc, got, _ = flow(True, t)
+        peer_keys = lambda: arrived(
+            kv_rows(kv, zc, ox), kv_recv.at[p, 1, t], kv_send.at[p, 1, t], x_peer
+        )
+
         def head(h, carry):
+            rows_in = at(zc * plane, plane, 128)
             scores = lax.dot_general(
-                qs[h], kv[:, pl.ds(0, HEAD_DIM)], (((1,), (1,)), ((), ())),
+                qs[h], kv[rows_in, pl.ds(0, HEAD_DIM)], (((1,), (1,)), ((), ())),
                 preferred_element_type=jnp.float32,
             )
-            scores = scores * exp_factor + mask[...]
-            probs = jnp.exp2(scores - jnp.max(scores, axis=-1, keepdims=True))
-            total = jnp.sum(probs, axis=-1, keepdims=True)
+            scores = scores + mask[:, rows_in]
+            top = jnp.max(scores, axis=-1, keepdims=True)
+            wide = (tok, HEAD_DIM)
+            if t:
+                top = jnp.maximum(top, tops[h, :, 0:1])
+            probs = jnp.exp2(scores - top)
+            total = jnp.broadcast_to(jnp.sum(probs, axis=-1, keepdims=True), wide)
             summed = jnp.dot(
-                probs.astype(jnp.bfloat16), kv[:, pl.ds(HEAD_DIM, HEAD_DIM)],
+                probs.astype(jnp.bfloat16), kv[rows_in, pl.ds(HEAD_DIM, HEAD_DIM)],
                 preferred_element_type=jnp.float32,
             )
-            ctx[:, at(c * qh + h * HEAD_DIM, HEAD_DIM, 128)] = (summed / total).astype(jnp.bfloat16)
+            top = jnp.broadcast_to(top, wide)
+            if t:
+                fade = jnp.exp2(tops[h] - top)
+                total += sums[h] * fade
+                summed += mixed[h] * fade
+            tops[h] = top
+            sums[h] = total
+            mixed[h] = summed
             return carry
 
-        lax.fori_loop(lo, hi, head, 0)
+        if t:
+            @pl.when(got)
+            def _():
+                peer_keys()
+                lax.fori_loop(0, group, head, 0)
+        else:
+            pl.when(x > ox)(peer_keys)
+            lax.fori_loop(0, group, head, 0)
+
+    def finish_heads(ctx):
+        def head(h, carry):
+            cols = at(c * qh + h * HEAD_DIM, HEAD_DIM, 128)
+            ctx[:, cols] = (mixed[h] / sums[h]).astype(jnp.bfloat16)
+            return carry
+
+        lax.fori_loop(0, group, head, 0)
 
     def share_ctx(p, ctx):
         ref = ctx.at[:, at(c * qh, qh, 128)]
@@ -415,18 +444,45 @@
             wide + jnp.dot(ctx[...], wouts[j][...], preferred_element_type=jnp.float32)
         ).astype(jnp.bfloat16)
 
-    def give(p, half, out):
-        cols = at(c * oh, oh, 128)
+    def heads_out(ctx, j, cc):
+        return jnp.dot(
+            ctx[:, at(cc * qh, qh, 128)], wouts[j][at(cc * qh, qh), :],
+            preferred_element_type=jnp.float32,
+        )
+
+    def project_own(src, ctx, j):
+        lo, width = chunks[j]
+        wide = src[:, at(c * oh + lo, width, 128)].astype(jnp.float32)
+        partial[:, pl.ds(lo, width)] = wide + heads_out(ctx, j, c)
+
+    def project_other(ctx, half, j):
+        cols = pl.ds(*chunks[j])
+        half[:, cols] = (partial[:, cols] + heads_out(ctx, j, oc)).astype(jnp.bfloat16)
+
+    n_out = len(chunks)
+    own_copies = []
+
+    def give(p, half, out, j):
+        lo, width = chunks[j]
+        i = 10 + p * n_out + j
+        cols = at(c * oh + lo, width, 128)
+        cols_in = pl.ds(lo, width)
         send(
-            half.at[at(oc * rows, rows)], out.at[:, cols], cx_send.at[10 + p], cx_recv.at[10 + p],
+            half.at[at(oc * rows, rows), cols_in], out.at[:, cols], cx_send.at[i], cx_recv.at[i],
             partner,
         )
-        copy = pltpu.make_async_copy(half.at[mine], out.at[:, cols], loc_sem.at[8 + p])
+        copy = pltpu.make_async_copy(
+            half.at[mine, cols_in], out.at[:, cols], loc_sem.at[8 + p * n_out + j]
+        )
         copy.start()
-        return copy
-
-    def given(p, out):
-        arrived(out.at[:, at(oc * oh, oh, 128)], cx_recv.at[10 + p], cx_send.at[10 + p], partner)
+        own_copies.append(copy)
+
+    def given(p, out, j):
+        lo, width = chunks[j]
+        i = 10 + p * n_out + j
+        arrived(
+            out.at[:, at(oc * oh + lo, width, 128)], cx_recv.at[i], cx_send.at[i], partner
+        )
 
     def pass_on(j):
         lo, width = chunks[j]
@@ -439,10 +495,10 @@
         lo, width = chunks[j]
         ref = xs2.at[:, at(c * oh + lo, width, 128)]
         pl.when(has_prev)(lambda: arrived(ref, ps_recv.at[j], ps_send.at[j], s_prev))
-        send(ref, ref, cx_send.at[12 + j], cx_recv.at[12 + j], partner, has_prev)
+        send(ref, ref, cx_send.at[10 + 2 * n_out + j], cx_recv.at[10 + 2 * n_out + j], partner, has_prev)
         pl.when(has_prev)(
             lambda: arrived(
-                xs2.at[:, at(oc * oh + lo, width, 128)], cx_recv.at[12 + j], cx_send.at[12 + j],
+                xs2.at[:, at(oc * oh + lo, width, 128)], cx_recv.at[10 + 2 * n_out + j], cx_send.at[10 + 2 * n_out + j],
                 partner,
             )
         )
@@ -451,6 +507,8 @@
     for i in range(3):
         own_ready(i)
     a_start(0)
+    own_ready(3)
+    a_start(1)
     tables(0)
     tables(1)
     make_mask(0)
@@ -458,7 +516,7 @@
     other_rows = at(oc * rows, rows)
     arrived(xs1.at[other_rows], cx_recv.at[6], cx_send.at[6], partner)
     scale_in(xs1, 0, oh, True)
-    for i in range(3, len(pieces)):
+    for i in range(4, len(pieces)):
         own_ready(i)
 
     def from_first():
@@ -468,9 +526,9 @@
     pl.when(first)(from_first)
     a_step(0, 1)
     a_step(0, 2)
-    a_start(1)
     a_step(0, 3)
     b_start(0)
+    a_start(2)
     b_steps(0)
     a_step(1, 1)
     gather_end(0)
@@ -479,31 +537,32 @@
     multiply(0, oh, 0, qh, True)
     finish_queries(0)
     a_step(1, 2)
-    a_start(2)
     a_step(1, 3)
     b_start(1)
+    a_start(3)
     b_steps(1)
     for t in range(1, PLANES):
         kv_step(0, kv1, t)
     a_step(2, 1)
-    keys_ready(0, kv1)
-    attend(kv1, ctx1, 0, 3)
+    attend(0, kv1, 0)
+    attend(0, kv1, 1)
     a_step(2, 2)
-    a_start(3)
-    attend(kv1, ctx1, 3, group)
-    share_ctx(0, ctx1)
+    a_step(3, 1)
+    attend(0, kv1, 2)
     a_step(2, 3)
     b_start(2)
+    a_step(3, 2)
+    attend(0, kv1, 3)
+    finish_heads(ctx1)
+    share_ctx(0, ctx1)
+    b_start(3)
     b_steps(2)
-    a_step(3, 1)
+    a_step(3, 3)
     make_mask(1)
     ctx_ready(0, ctx1)
     gather_end(1)
     project_out(xs1, ctx1, half1, 0)
     pass_on(0)
-    a_step(3, 2)
-    a_step(3, 3)
-    b_start(3)
     gather_end(2)
     project_out(xs1, ctx1, half1, 1)
     pass_on(1)
@@ -517,26 +576,34 @@
     gather_end(3)
     project_out(xs1, ctx1, half1, 2)
     pass_on(2)
-    out_copy1 = give(0, half1, out1_ref)
+    for j in range(n_out):
+        give(0, half1, out1_ref, j)
     passed(2)
     multiply(*chunks[2], qh, 2 * kh, False)
     finish_keys(1, kv2)
     multiply(*chunks[2], 0, qh, False)
     finish_queries(1)
-    for t in range(1, PLANES):
-        kv_step(1, kv2, t)
-    keys_ready(1, kv2)
-    attend(kv2, ctx2, 0, group)
+    kv_step(1, kv2, 1)
+    attend(1, kv2, 0)
+    kv_step(1, kv2, 2)
+    attend(1, kv2, 1)
+    kv_step(1, kv2, 3)
+    attend(1, kv2, 2)
+    attend(1, kv2, 3)
+    finish_heads(ctx2)
     share_ctx(1, ctx2)
+    for j in range(n_out):
+        project_own(xs2, ctx2, j)
     ctx_ready(1, ctx2)
-    for j in range(len(chunks)):
-        project_out(xs2, ctx2, half2, j)
-    out_copy2 = give(1, half2, out2_ref)
-
-    given(0, out1_ref)
-    given(1, out2_ref)
-    out_copy1.wait()
-    out_copy2.wait()
+    for j in range(n_out):
+        project_other(ctx2, half2, j)
+        give(1, half2, out2_ref, j)
+
+    for p, out in ((0, out1_ref), (1, out2_ref)):
+        for j in range(n_out):
+            given(p, out, j)
+    for copy in own_copies:
+        copy.wait()
     for copy, cond in sent:
         if cond is None:
             copy.wait_send()
@@ -593,6 +660,7 @@
             pltpu.VMEM((2, 2, tok, HEAD_DIM), f32),
             pltpu.VMEM((2, tok, HEAD_DIM), f32),
             pltpu.VMEM((HEADS // KV_HEADS, tok, HEAD_DIM), bf16),
+            *[pltpu.VMEM((HEADS // KV_HEADS, tok, HEAD_DIM), f32)] * 3,
             pltpu.VMEM((seq_len, 2 * HEAD_DIM), bf16),
             pltpu.VMEM((seq_len, 2 * HEAD_DIM), bf16),
             pltpu.VMEM((tok, seq_len), f32),
@@ -600,9 +668,10 @@
             pltpu.VMEM((tok, qw), bf16),
             pltpu.VMEM((tok, oh), bf16),
             pltpu.VMEM((tok, oh), bf16),
-            dma((10,)),
-            dma((15,)),
-            dma((15,)),
+            pltpu.VMEM((tok, oh), f32),
+            dma((8 + 2 * len(cuts),)),
+            dma((10 + 3 * len(cuts),)),
+            dma((10 + 3 * len(cuts),)),
             z_sems,
             z_sems,
             z_sems,

time: 211 us -> 212 us (level)
  no operation moved by 1% of the time
where the time goes in v3:
time: 212 us
  Pallas kernels  206 us (97%)
  local copies, waits for them, and re-layouts  3.74 us (2%)
    pallas_call x1, Pallas kernels, per_device(): pl.pallas_call(functools.partial(kernel, n_section, (rows, d, qw, kvw)),...  206 us

profile of v3, /device:TPU:29, one launch (start us, length us, event | category | flops | bytes accessed | tf_op | source)
XLA Modules:
  0.0 211.5 jit_solution(3238561484762783754)
XLA Ops:
  0.6 0.0 copy-start.1
  0.7 0.1 maximum_bitcast_fusion
  0.7 0.6 copy-done.1
  1.3 0.6 pad_maximum_fusion.freq_ref
  1.9 206.5 %two_sections.1 = (bf16[128,3584]{1,0:T(8,128)(2,1)}, bf16[128,3584]{1,0:T(8,128)(2,1)}) custom-call(bf16[128,3584]{1,0:T(8,128)(2,1)} %bitcast.9, bf16[128,3584]{1,0:T(8,128)(2,1)} %inc_ref.1, bf16[224,1792]{1,0:T(8,128)(2,1)} %bitcast.12, bf16[224,256]{1,0:T(8,128)(2,1)} %bitcast.14, bf16[224,256]{1,0:T(8,128)(2,1)} %bitcast.15, ...), custom_call_target="tpu_custom_call" | custom-call | tf_op jit(solution)/shard_map/two_sections/pallas_call | solution.py:647
  208.4 0.0 copy-start
  208.4 2.2 %copy.16 = bf16[1,128,3584]{2,1,0:T(8,128)(2,1)} copy(bf16[1,128,3584]{2,1,0:T(8,128)(2,1)} %bitcast.11) | data formatting | bytes 1835008
  210.6 0.0 copy-done
  210.6 0.9 copy.17
  (1 shorter events, 0.0 us)
Async XLA Ops:
  0.6 0.7 copy-start.1
  208.4 2.3 %copy-start = (bf16[128,3584]{1,0:T(8,128)(2,1)S(1)}, bf16[128,3584]{1,0:T(8,128)(2,1)}, u32[]{:S(2)}) copy-start(bf16[128,3584]{1,0:T(8,128)(2,1)} %get-tuple-element.5) | copy-start | bytes 2752516

commit v4 on v3

--- a/solution.py
+++ b/solution.py
@@ -3,6 +3,7 @@
 
 import jax
 import jax.numpy as jnp
+import numpy as np
 from jax import lax
 from jax.experimental import pallas as pl
 from jax.experimental.pallas import tpu as pltpu
@@ -37,7 +38,8 @@
     pos_ref,
     out1_ref,
     out2_ref,
-    wqkv,
+    wkv,
+    wquery,
     wout_a,
     wout_b,
     wout_c,
@@ -156,13 +158,13 @@
         chunks.append((low, buf.shape[1]))
         low += buf.shape[1]
     pieces = [
-        (wq_ref, wqkv, row0, orow0, wr, qh, 0, 0),
-        (wk_ref, wqkv, row0, orow0, wr, kh, 0, qh),
-        (wv_ref, wqkv, row0, orow0, wr, kh, 0, qh + kh),
+        (wk_ref, wkv, row0, orow0, wr, kh, 0, 0),
+        (wv_ref, wkv, row0, orow0, wr, kh, 0, kh),
+        (wq_ref, wquery, row0, orow0, wr, qh, 0, 0),
     ] + [
         (wo_ref, buf, wrow0, worow0, wor, oh, lo, 0) for buf, (lo, _) in zip(wouts, chunks)
     ]
-    widths = [qh, kh, kh] + [w for _, w in chunks]
+    widths = [kh, kh, qh] + [w for _, w in chunks]
     local = []
     for i, (src, dst, r0, _, n, part, lo, col) in enumerate(pieces):
         width = widths[i]
@@ -191,9 +193,9 @@
         local[i].wait()
         arrived(dst.at[at(r1, n), pl.ds(col, widths[i])], cx_recv.at[i], cx_send.at[i], partner)
 
-    bufs = [wqkv] + wouts
-    shard = [CORES * wr] + [CORES * wor] * len(wouts)
-    tails = [80] + [32] * len(wouts)
+    bufs = [wkv, wquery] + wouts
+    shard = [CORES * wr] * 2 + [CORES * wor] * len(wouts)
+    tails = [80] * 2 + [32] * len(wouts)
 
     def apart(w, zz, xx):
         return bufs[w].at[at((zz * CHIPS_X + xx) * shard[w], shard[w] - tails[w])]
@@ -316,14 +318,14 @@
 
         lax.fori_loop(0, tok // 32, body, 0)
 
-    def multiply(lo, width, col, n, start):
+    def multiply(lo, width, weights, start):
         total = 0.0
         for cc in range(CORES):
             part = pl.ds(cc * oh + lo, width)
             total += jnp.dot(
-                hidden[:, part], wqkv[part, pl.ds(col, n)], preferred_element_type=jnp.float32
+                hidden[:, part], weights[part, :], preferred_element_type=jnp.float32
             )
-        cols = pl.ds(col, n)
+        cols = pl.ds(0, qh) if weights is wquery else pl.ds(qh, 2 * kh)
         acc[:, cols] = total if start else acc[:, cols] + total
 
     def row_factor():
@@ -504,19 +506,24 @@
         )
         scale_in(xs2, lo, width, j == 0)
 
-    for i in range(3):
+    for i in range(2):
         own_ready(i)
     a_start(0)
-    own_ready(3)
+    own_ready(2)
     a_start(1)
     tables(0)
-    tables(1)
-    make_mask(0)
     local[6].wait()
     other_rows = at(oc * rows, rows)
     arrived(xs1.at[other_rows], cx_recv.at[6], cx_send.at[6], partner)
     scale_in(xs1, 0, oh, True)
-    for i in range(4, len(pieces)):
+    a_step(0, 1)
+    make_mask(0)
+    a_step(0, 2)
+    tables(1)
+    a_step(0, 3)
+    b_start(0)
+    b_steps(0)
+    for i in range(3, len(pieces)):
         own_ready(i)
 
     def from_first():
@@ -524,64 +531,71 @@
         arrived(xs2.at[other_rows], cx_recv.at[7], cx_send.at[7], partner)
 
     pl.when(first)(from_first)
-    a_step(0, 1)
-    a_step(0, 2)
-    a_step(0, 3)
-    b_start(0)
-    a_start(2)
-    b_steps(0)
     a_step(1, 1)
     gather_end(0)
-    multiply(0, oh, qh, 2 * kh, True)
+    multiply(0, oh, wkv, True)
     finish_keys(0, kv1)
-    multiply(0, oh, 0, qh, True)
+    a_step(1, 2)
+    a_start(2)
+    kv_step(0, kv1, 1)
+    a_step(1, 3)
+    kv_step(0, kv1, 2)
+    b_start(1)
+    b_steps(1)
+    kv_step(0, kv1, 3)
+    a_step(2, 1)
+    a_start(3)
+    gather_end(1)
+    multiply(0, oh, wquery, True)
     finish_queries(0)
-    a_step(1, 2)
-    a_step(1, 3)
-    b_start(1)
-    a_start(3)
-    b_steps(1)
-    for t in range(1, PLANES):
-        kv_step(0, kv1, t)
-    a_step(2, 1)
+    a_step(2, 2)
     attend(0, kv1, 0)
     attend(0, kv1, 1)
-    a_step(2, 2)
-    a_step(3, 1)
-    attend(0, kv1, 2)
     a_step(2, 3)
     b_start(2)
-    a_step(3, 2)
+    attend(0, kv1, 2)
+    b_step(2, 1)
     attend(0, kv1, 3)
     finish_heads(ctx1)
     share_ctx(0, ctx1)
-    b_start(3)
-    b_steps(2)
-    a_step(3, 3)
-    make_mask(1)
+    b_step(2, 2)
+    b_step(2, 3)
+    a_step(3, 1)
+    a_start(4)
     ctx_ready(0, ctx1)
-    gather_end(1)
+    gather_end(2)
     project_out(xs1, ctx1, half1, 0)
     pass_on(0)
-    gather_end(2)
+    a_step(3, 2)
+    make_mask(1)
+    a_step(3, 3)
+    b_start(3)
+    a_step(4, 1)
+    b_step(3, 1)
+    a_step(4, 2)
+    b_step(3, 2)
+    b_step(3, 3)
+    a_step(4, 3)
+    b_start(4)
+    gather_end(3)
     project_out(xs1, ctx1, half1, 1)
     pass_on(1)
+    b_steps(4)
     passed(0)
-    multiply(*chunks[0], qh, 2 * kh, True)
-    multiply(*chunks[0], 0, qh, True)
-    b_steps(3)
-    passed(1)
-    multiply(*chunks[1], qh, 2 * kh, False)
-    multiply(*chunks[1], 0, qh, False)
-    gather_end(3)
+    multiply(*chunks[0], wkv, True)
+    multiply(*chunks[0], wquery, True)
+    gather_end(4)
     project_out(xs1, ctx1, half1, 2)
     pass_on(2)
     for j in range(n_out):
         give(0, half1, out1_ref, j)
+    passed(1)
+    multiply(*chunks[1], wkv, False)
+    multiply(*chunks[1], wquery, False)
     passed(2)
-    multiply(*chunks[2], qh, 2 * kh, False)
+    multiply(*chunks[2], wkv, False)
     finish_keys(1, kv2)
-    multiply(*chunks[2], 0, qh, False)
+    multiply(*chunks[2], wquery, False)
     finish_queries(1)
     kv_step(1, kv2, 1)
     attend(1, kv2, 0)
@@ -632,17 +646,18 @@
     tok = rows * CORES
     seq_len = column_ids.shape[1]
     half = HEAD_DIM // 2
-    freqs = THETA ** (-(jnp.arange(half, dtype=jnp.float32) * 2.0) / HEAD_DIM)
-    signs = jnp.ones((half,), jnp.float32)
-    freqs = jnp.stack([jnp.concatenate([freqs, freqs]), jnp.concatenate([-signs, signs])])
-    cuts = [oh * 3 // 7, oh * 5 // 14, oh * 3 // 14]
+    freqs = THETA ** (-(np.arange(half) * 2.0) / HEAD_DIM)
+    signs = np.ones((half,))
+    freqs = np.stack([np.concatenate([freqs, freqs]), np.concatenate([-signs, signs])])
+    freqs = freqs.astype(np.float32)
+    cuts = [oh * 3 // 7, oh * 3 // 7, oh // 7]
     bf16, f32 = jnp.bfloat16, jnp.float32
     anywhere = pl.BlockSpec(memory_space=pl.ANY)
     vmem = pl.BlockSpec(memory_space=pltpu.VMEM)
     dma = pltpu.SemaphoreType.DMA
     shape = jax.ShapeDtypeStruct((rows, d), bf16)
     width = qh + 2 * kh
-    jobs = 1 + len(cuts)
+    jobs = 2 + len(cuts)
     z_sems = dma((jobs, PLANES - 1, 3))
     out1, out2 = pl.pallas_call(
         functools.partial(kernel, n_section, (rows, d, qw, kvw)),
@@ -650,7 +665,8 @@
         in_specs=[anywhere] * 6 + [vmem] * 7,
         out_specs=(anywhere, anywhere),
         scratch_shapes=[
-            pltpu.VMEM((d, width), bf16),
+            pltpu.VMEM((d, 2 * kh), bf16),
+            pltpu.VMEM((d, qh), bf16),
             *[pltpu.VMEM((qw, cut), bf16) for cut in cuts],
             pltpu.VMEM((tok, d), bf16),
             pltpu.VMEM((tok, d), bf16),

time: 212 us -> 210 us (level)
  no operation moved by 1% of the time
where the time goes in v4:
time: 210 us
  Pallas kernels  206 us (98%)
  local copies, waits for them, and re-layouts  3.17 us (2%)
    pallas_call x1, Pallas kernels, per_device(): pl.pallas_call(functools.partial(kernel, n_section, (rows, d, qw, kvw)),...  206 us

profile of v4, /device:TPU:29, one launch (start us, length us, event | category | flops | bytes accessed | tf_op | source)
XLA Modules:
  0.0 210.0 jit_solution(6787371495711368353)
XLA Ops:
  0.6 206.2 %two_sections.1 = (bf16[128,3584]{1,0:T(8,128)(2,1)}, bf16[128,3584]{1,0:T(8,128)(2,1)}) custom-call(bf16[128,3584]{1,0:T(8,128)(2,1)} %bitcast.7, bf16[128,3584]{1,0:T(8,128)(2,1)} %inc_ref.1, bf16[224,1792]{1,0:T(8,128)(2,1)} %bitcast.10, bf16[224,256]{1,0:T(8,128)(2,1)} %bitcast.12, bf16[224,256]{1,0:T(8,128)(2,1)} %bitcast.13, ...), custom_call_target="tpu_custom_call" | custom-call | tf_op jit(solution)/shard_map/two_sections/pallas_call | solution.py:662
  206.8 0.0 copy-start
  206.8 2.2 %copy.17 = bf16[1,128,3584]{2,1,0:T(8,128)(2,1)} copy(bf16[1,128,3584]{2,1,0:T(8,128)(2,1)} %bitcast.9) | data formatting | bytes 1835008
  209.1 0.0 copy-done
  209.1 0.9 copy.18
Async XLA Ops:
  206.8 2.3 %copy-start = (bf16[128,3584]{1,0:T(8,128)(2,1)S(1)}, bf16[128,3584]{1,0:T(8,128)(2,1)}, u32[]{:S(2)}) copy-start(bf16[128,3584]{1,0:T(8,128)(2,1)} %get-tuple-element.5) | copy-start | bytes 2752516

commit v5 on v4

--- a/solution.py
+++ b/solution.py
@@ -254,9 +254,9 @@
                 if t < PLANES - 1:
                     z_send(ref, w, t, part, up, on)
 
-    def b_steps(w):
-        for t in range(1, PLANES):
-            b_step(w, t)
+    def step(w, t):
+        a_step(w, t)
+        b_step(w, t)
 
     def gather_end(w):
         arrived(apart(w, z, ox), xl_recv.at[w, 1], xl_send.at[w, 1], x_peer)
@@ -361,14 +361,14 @@
     def finish_queries(p):
         factor = row_factor()
 
-        def head(h, carry):
-            cols = at(h * HEAD_DIM, HEAD_DIM, 128)
+        def head(h):
+            cols = pl.ds(h * HEAD_DIM, HEAD_DIM)
             query_bias = bq_ref[:, at(c * qh + h * HEAD_DIM, HEAD_DIM, 128)]
             turned = turn(p, acc[:, cols] * factor + query_bias)
             qs[h] = (turned * exp_factor).astype(jnp.bfloat16)
-            return carry
-
-        lax.fori_loop(0, group, head, 0)
+
+        for h in range(group):
+            head(h)
 
     def kv_step(p, kv, t):
         zc, got, on = flow(True, t)
@@ -388,49 +388,49 @@
             kv_rows(kv, zc, ox), kv_recv.at[p, 1, t], kv_send.at[p, 1, t], x_peer
         )
 
-        def head(h, carry):
+        def heads():
             rows_in = at(zc * plane, plane, 128)
+            all_rows = (group * tok, HEAD_DIM)
+            wide = (group, tok, HEAD_DIM)
             scores = lax.dot_general(
-                qs[h], kv[rows_in, pl.ds(0, HEAD_DIM)], (((1,), (1,)), ((), ())),
-                preferred_element_type=jnp.float32,
+                qs[...].reshape(all_rows), kv[rows_in, pl.ds(0, HEAD_DIM)],
+                (((1,), (1,)), ((), ())), preferred_element_type=jnp.float32,
             )
-            scores = scores + mask[:, rows_in]
+            scores = scores.reshape(group, tok, plane) + mask[:, rows_in][None]
             top = jnp.max(scores, axis=-1, keepdims=True)
-            wide = (tok, HEAD_DIM)
             if t:
-                top = jnp.maximum(top, tops[h, :, 0:1])
+                top = jnp.maximum(top, tops[:, :, 0:1])
             probs = jnp.exp2(scores - top)
             total = jnp.broadcast_to(jnp.sum(probs, axis=-1, keepdims=True), wide)
             summed = jnp.dot(
-                probs.astype(jnp.bfloat16), kv[rows_in, pl.ds(HEAD_DIM, HEAD_DIM)],
-                preferred_element_type=jnp.float32,
-            )
+                probs.astype(jnp.bfloat16).reshape(group * tok, plane),
+                kv[rows_in, pl.ds(HEAD_DIM, HEAD_DIM)], preferred_element_type=jnp.float32,
+            ).reshape(wide)
             top = jnp.broadcast_to(top, wide)
             if t:
-                fade = jnp.exp2(tops[h] - top)
-                total += sums[h] * fade
-                summed += mixed[h] * fade
-            tops[h] = top
-            sums[h] = total
-            mixed[h] = summed
-            return carry
+                fade = jnp.exp2(tops[...] - top)
+                total += sums[...] * fade
+                summed += mixed[...] * fade
+            tops[...] = top
+            sums[...] = total
+            mixed[...] = summed
 
         if t:
             @pl.when(got)
             def _():
                 peer_keys()
-                lax.fori_loop(0, group, head, 0)
+                heads()
         else:
             pl.when(x > ox)(peer_keys)
-            lax.fori_loop(0, group, head, 0)
+            heads()
 
     def finish_heads(ctx):
-        def head(h, carry):
+        def head(h):
             cols = at(c * qh + h * HEAD_DIM, HEAD_DIM, 128)
             ctx[:, cols] = (mixed[h] / sums[h]).astype(jnp.bfloat16)
-            return carry
-
-        lax.fori_loop(0, group, head, 0)
+
+        for h in range(group):
+            head(h)
 
     def share_ctx(p, ctx):
         ref = ctx.at[:, at(c * qh, qh, 128)]
@@ -516,13 +516,11 @@
     other_rows = at(oc * rows, rows)
     arrived(xs1.at[other_rows], cx_recv.at[6], cx_send.at[6], partner)
     scale_in(xs1, 0, oh, True)
-    a_step(0, 1)
+    b_start(0)
+    step(0, 1)
     make_mask(0)
-    a_step(0, 2)
+    step(0, 2)
     tables(1)
-    a_step(0, 3)
-    b_start(0)
-    b_steps(0)
     for i in range(3, len(pieces)):
         own_ready(i)
 
@@ -531,56 +529,49 @@
         arrived(xs2.at[other_rows], cx_recv.at[7], cx_send.at[7], partner)
 
     pl.when(first)(from_first)
-    a_step(1, 1)
+    step(0, 3)
+    b_start(1)
     gather_end(0)
     multiply(0, oh, wkv, True)
     finish_keys(0, kv1)
-    a_step(1, 2)
+    step(1, 1)
     a_start(2)
     kv_step(0, kv1, 1)
-    a_step(1, 3)
+    step(1, 2)
     kv_step(0, kv1, 2)
-    b_start(1)
-    b_steps(1)
+    b_start(2)
+    step(1, 3)
     kv_step(0, kv1, 3)
-    a_step(2, 1)
     a_start(3)
+    step(2, 1)
     gather_end(1)
     multiply(0, oh, wquery, True)
     finish_queries(0)
-    a_step(2, 2)
+    step(2, 2)
     attend(0, kv1, 0)
+    b_start(3)
     attend(0, kv1, 1)
-    a_step(2, 3)
-    b_start(2)
+    step(2, 3)
+    a_start(4)
     attend(0, kv1, 2)
-    b_step(2, 1)
+    step(3, 1)
     attend(0, kv1, 3)
     finish_heads(ctx1)
     share_ctx(0, ctx1)
-    b_step(2, 2)
-    b_step(2, 3)
-    a_step(3, 1)
-    a_start(4)
+    b_start(4)
+    step(3, 2)
     ctx_ready(0, ctx1)
     gather_end(2)
     project_out(xs1, ctx1, half1, 0)
     pass_on(0)
-    a_step(3, 2)
+    step(4, 1)
+    step(3, 3)
     make_mask(1)
-    a_step(3, 3)
-    b_start(3)
-    a_step(4, 1)
-    b_step(3, 1)
-    a_step(4, 2)
-    b_step(3, 2)
-    b_step(3, 3)
-    a_step(4, 3)
-    b_start(4)
+    step(4, 2)
     gather_end(3)
     project_out(xs1, ctx1, half1, 1)
     pass_on(1)
-    b_steps(4)
+    step(4, 3)
     passed(0)
     multiply(*chunks[0], wkv, True)
     multiply(*chunks[0], wquery, True)
@@ -650,7 +641,7 @@
     signs = np.ones((half,))
     freqs = np.stack([np.concatenate([freqs, freqs]), np.concatenate([-signs, signs])])
     freqs = freqs.astype(np.float32)
-    cuts = [oh * 3 // 7, oh * 3 // 7, oh // 7]
+    cuts = [oh * 3 // 7, oh * 5 // 14, oh * 3 // 14]
     bf16, f32 = jnp.bfloat16, jnp.float32
     anywhere = pl.BlockSpec(memory_space=pl.ANY)
     vmem = pl.BlockSpec(memory_space=pltpu.VMEM)

time: 210 us -> 203 us (0.967)
  Pallas kernels: 206 us -> 199 us
    pallas_call x1, Pallas kernels: 206 us -> 199 us  [per_device(): pl.pallas_call(functools.partial(kernel, n_section, (rows, d, qw, kvw)),...]
where the time goes in v5:
time: 203 us
  Pallas kernels  199 us (98%)
  local copies, waits for them, and re-layouts  3.17 us (2%)
    pallas_call x1, Pallas kernels, per_device(): pl.pallas_call(functools.partial(kernel, n_section, (rows, d, qw, kvw)),...  199 us

profile of v5, /device:TPU:29, one launch (start us, length us, event | category | flops | bytes accessed | tf_op | source)
XLA Modules:
  0.0 202.8 jit_solution(5971895537641904036)
XLA Ops:
  0.6 199.0 %two_sections.1 = (bf16[128,3584]{1,0:T(8,128)(2,1)}, bf16[128,3584]{1,0:T(8,128)(2,1)}) custom-call(bf16[128,3584]{1,0:T(8,128)(2,1)} %bitcast.7, bf16[128,3584]{1,0:T(8,128)(2,1)} %inc_ref.1, bf16[224,1792]{1,0:T(8,128)(2,1)} %bitcast.10, bf16[224,256]{1,0:T(8,128)(2,1)} %bitcast.12, bf16[224,256]{1,0:T(8,128)(2,1)} %bitcast.13, ...), custom_call_target="tpu_custom_call" | custom-call | tf_op jit(solution)/shard_map/two_sections/pallas_call | solution.py:653
  199.7 0.0 copy-start
  199.7 2.2 %copy.17 = bf16[1,128,3584]{2,1,0:T(8,128)(2,1)} copy(bf16[1,128,3584]{2,1,0:T(8,128)(2,1)} %bitcast.9) | data formatting | bytes 1835008
  201.9 0.0 copy-done
  201.9 0.9 copy.18
Async XLA Ops:
  199.7 2.3 %copy-start = (bf16[128,3584]{1,0:T(8,128)(2,1)S(1)}, bf16[128,3584]{1,0:T(8,128)(2,1)}, u32[]{:S(2)}) copy-start(bf16[128,3584]{1,0:T(8,128)(2,1)} %get-tuple-element.5) | copy-start | bytes 2752516
